TPU v7x, 32 devices: a whole 2x2x4 slice. The times are simulated.
32 devices in a mesh: theta: 8 (over y, x, core), span: 4 (over z).
Axes of the slice: x: 2, y: 2, z: 4, core: 2. Of those that a mesh axis runs over, the one named last changes fastest.
Arguments:
- velocity: float32 [3, 9, 64, 8192], P(None, None, 'theta', 'span'), may hold values from -6 to 6
- pressure: float32 [9, 64, 8192], P(None, 'theta', 'span'), may hold values from -6 to 6
- diffusivity: float32 [64, 8192], P('theta', 'span'), may hold values from 0.3 to 3
- live_blocks: int32 [8, 4], P('theta', 'span'), may hold values from 1 to 8
- owner_map: int32 [64, 8192], P('theta', 'span'), may hold values from 0 to 511, as said below
- coarse_diag: float32 [16, 512], P('theta', 'span'), may hold values from 0.5 to 4
Outputs:
- predicted: float32 [3, 9, 64, 8192], P(None, None, 'theta', 'span')
- correction: float32 [9, 64, 8192], P(None, 'theta', 'span')
Inputs may be any that keep to these rules, and one draw needn't show every extreme that they name: owner_map[a, r] is r // 16, or one less where r mod 16 is 0, or one more where r mod 16 is 15, never leaving the columns (r // 2048) * (128) to (r // 2048 + 1) * 128 - 1.
All inputs are finite; a program needn't handle non-finite values.
Results may differ from a plain program's by a relative error of at most 0.0001.
Values sent between devices are 32-bit elements; how exact they have to be, the bound alone decides.
A program may use at most 128 MiB of HBM per device.

v0:
```python
import math

import jax
import jax.numpy as jnp
from jax import lax
from jax.sharding import PartitionSpec as P

BLOCKS = 8
CSWEEPS = 4


step_size = 0.2
viscosity = 0.5
swirl = 0.5
frequency = 0.3
relax_fine = 0.2
relax_coarse = 0.8


def padded(block, sides, width, periodic):
    for axis, dim in sides:
        count = lax.axis_size(axis)
        forward = [(i, i + 1) for i in range(count - 1)]
        if periodic:
            forward.append((count - 1, 0))
        backward = [(target, source) for source, target in forward]
        low = lax.ppermute(
            lax.slice_in_dim(block, block.shape[dim] - width, None, axis=dim), axis, forward
        )
        high = lax.ppermute(lax.slice_in_dim(block, 0, width, axis=dim), axis, backward)
        block = jnp.concatenate([low, block, high], axis=dim)
    return block


def spectral_matrix(count):
    rows = jnp.arange(count)[:, None]
    cols = jnp.arange(count)[None, :]
    gap = (rows - cols).astype(jnp.float32)
    parity = 1.0 - 2.0 * ((rows - cols) % 2).astype(jnp.float32)
    safe = jnp.where(rows == cols, 1.0, jnp.sin(math.pi * gap / count))
    return jnp.where(rows == cols, 0.0, frequency * 0.5 * parity / safe)


def coarse_sweeps(rhs, denom, neighbours):
    coarse = relax_coarse * rhs / denom
    for sweep in range(CSWEEPS - 1):
        applied = denom * coarse - neighbours(coarse)
        coarse = coarse + relax_coarse * (rhs - applied) / denom
    return coarse


def azimuth_pair(field):
    extended = padded(field, (("theta", 2),), 1, True)
    return (extended[:, :, 2:], extended[:, :, :-2])


def radial_pair(field):
    extended = padded(field, (("span", 3),), 1, False)
    return (extended[:, :, :, 2:], extended[:, :, :, :-2])


def shard_neighbours(field):
    beside_all = padded(field[None], (("theta", 2),), 1, True)
    beside = padded(field[None], (("span", 3),), 1, False)
    return beside_all[0, :, 2:] + beside_all[0, :, :-2] + beside[0, :, :, 2:] + beside[0, :, :, :-2]


def block_total(field, cplanes, ccells):
    ntime = field.shape[0]
    return field.reshape(ntime, cplanes, 4, ccells, 16).sum(axis=(2, 4))


def shift_lower(field):
    zero = jnp.zeros_like(field[..., :1])
    return jnp.concatenate([field[..., 1:], zero], -1)


def shift_higher(field):
    zero = jnp.zeros_like(field[..., :1])
    return jnp.concatenate([zero, field[..., :-1]], -1)


def expand(field, planes, cells):
    ntime, cplanes, ccells = field.shape
    wide = jnp.broadcast_to(field[:, :, None, :, None], (ntime, cplanes, 4, ccells, 16))
    return wide.reshape(ntime, planes, cells)


def shards(velocity, pressure, diffusivity, live_blocks, owner_map, coarse_diag):
    ncomp, ntime, planes, cells = velocity.shape
    cplanes = planes // 4
    ccells = cells // 16
    live = live_blocks.reshape(())
    fluid = (jnp.arange(cells) < live * (cells // BLOCKS)).astype(jnp.float32)
    coupling = spectral_matrix(ntime)
    source = jnp.einsum("nm,cmar->cnar", coupling, velocity, precision=lax.Precision.HIGHEST)
    stacked = jnp.concatenate([velocity, pressure[None]], 0)
    az_next, az_prev = azimuth_pair(stacked)
    rad_next, rad_prev = radial_pair(stacked)
    grads = jnp.stack(
        [
            0.5 * (az_next[3] - az_prev[3]),
            0.5 * (rad_next[3] - rad_prev[3]),
            jnp.zeros_like(pressure),
        ],
        0,
    )
    lap = az_next[:3] + az_prev[:3] + rad_next[:3] + rad_prev[:3] - 4.0 * velocity
    upwind = velocity - az_prev[:3]
    predicted = fluid * (
        velocity + step_size * (viscosity * diffusivity * lap - swirl * upwind - source - grads)
    )
    first_next, first_prev = azimuth_pair(predicted[0:1])
    second_next, second_prev = radial_pair(predicted[1:2])
    imbalance = fluid * (0.5 * (first_next - first_prev) + 0.5 * (second_next - second_prev))
    smoothed = relax_fine * imbalance
    sm_next_a, sm_prev_a = azimuth_pair(smoothed)
    sm_next_r, sm_prev_r = radial_pair(smoothed)
    beside_all = sm_next_a + sm_prev_a + sm_next_r + sm_prev_r
    applied = fluid * (4.0 * smoothed - beside_all) + (1.0 - fluid) * smoothed
    remainder = (imbalance - applied)[0]
    offset = owner_map - lax.axis_index("span") * ccells - (jnp.arange(cells) // 16)[None, :]
    to_lower = (offset == -1).astype(jnp.float32)
    to_higher = (offset == 1).astype(jnp.float32)
    moved_lower = block_total(remainder * to_lower, cplanes, ccells)
    moved_higher = block_total(remainder * to_higher, cplanes, ccells)
    coarse_rhs = (
        block_total(remainder, cplanes, ccells)
        - moved_lower
        - moved_higher
        + shift_lower(moved_lower)
        + shift_higher(moved_higher)
    )
    coarse = coarse_sweeps(coarse_rhs, 4.0 + coarse_diag, shard_neighbours)
    lifted = jnp.where(
        offset == -1,
        expand(shift_higher(coarse), planes, cells),
        jnp.where(
            offset == 1, expand(shift_lower(coarse), planes, cells), expand(coarse, planes, cells)
        ),
    )
    correction = fluid * (smoothed[0] + lifted)
    return (predicted, correction)


def solution(mesh):
    return jax.shard_map(
        shards,
        mesh=mesh,
        in_specs=(
            P(None, None, "theta", "span"),
            P(None, "theta", "span"),
            P("theta", "span"),
            P("theta", "span"),
            P("theta", "span"),
            P("theta", "span"),
        ),
        out_specs=(P(None, None, "theta", "span"), P(None, "theta", "span")),
        check_vma=False,
    )
```

profile of v0, /device:TPU:0, one launch (start us, length us, event | category | flops | bytes accessed | tf_op | source)
XLA Modules:
  0.0 124.1 jit_solution(15523895974551340576)
XLA Ops:
  0.6 2.6 %copy.21 = f32[3,9,8,2048]{3,1,2,0:T(8,128)S(1)} copy(f32[3,9,8,2048]{3,2,1,0:T(8,128)} %param.6) | data formatting | bytes 3538944 | tf_op args[0]
  3.3 0.4 copy.39
  3.7 1.2 pad_maximum_fusion.10
  4.9 3.3 %collective-permute-start = (f32[4,9,1,2048]{3,1,2,0:T(8,128)}, f32[4,9,1,2048]{3,1,2,0:T(8,128)}, u32[]{:S(2)}, u32[]{:S(2)}) collective-permute-start(f32[4,9,1,2048]{3,1,2,0:T(8,128)} %get-tuple-element.22), channel_id=1, source_target_pairs={{4,0},{8,4},{12,8},{16,12},{20,16},{24,20},{28,24},{0,28},{5,1},{9... | collective-permute-start | bytes 884744 | tf_op jit(solution)/shard_map/ppermute | solution.py:30
  8.2 0.9 pad_maximum_fusion.13
  9.1 1.3 %collective-permute-start.2 = (f32[4,9,8,1]{3,1,2,0:T(8,128)}, f32[4,9,8,1]{3,1,2,0:T(8,128)S(1)}, u32[]{:S(2)}, u32[]{:S(2)}) collective-permute-start(f32[4,9,8,1]{3,1,2,0:T(8,128)} %get-tuple-element.25), channel_id=1, source_target_pairs={{1,0},{2,1},{3,2},{5,4},{6,5},{7,6},{9,8},{10,9},{11,10},{13,12},{... | collective-permute-start | bytes 3464 | tf_op jit(solution)/shard_map/ppermute | solution.py:30
  10.4 5.2 %collective-permute-start.3 = (f32[4,9,8,1]{3,1,2,0:T(8,128)}, f32[4,9,8,1]{3,1,2,0:T(8,128)}, u32[]{:S(2)}, u32[]{:S(2)}) collective-permute-start(f32[4,9,8,1]{3,1,2,0:T(8,128)} %get-tuple-element.26), channel_id=1, source_target_pairs={{0,1},{1,2},{2,3},{4,5},{5,6},{6,7},{8,9},{9,10},{10,11},{12,13},{... | collective-permute-start | bytes 3464 | tf_op jit(solution)/shard_map/ppermute | solution.py:27
  16.3 0.6 fusion.61
  16.9 1.3 %broadcast_add_fusion = f32[2,128]{1,0:T(2,128)} fusion(f32[2,128]{1,0:T(2,128)} %param.11), kind=kLoop, calls=%fused_computation.130 | loop fusion | flops 256 | bytes 2048 | tf_op jit(solution)/shard_map/add | solution.py:134
  18.2 1.5 %fusion.85 = (f32[8,2048]{1,0:T(8,128)}, pred[8,2048]{1,0:T(8,128)(4,1)}, f32[8,2048]{1,0:T(8,128)S(1)}, pred[8,2048]{1,0:T(8,128)(4,1)}) fusion(s32[2048]{0:T(1024)S(1)} %add_select_fusion, s32[8,2048]{1,0:T(8,128)} %param.10, s32[]{:T(128)S(6)} %mul.219), kind=kLoop, calls=%fused_computation.141 | loop fusion | flops 98304 | bytes 237572 | tf_op jit(solution)/shard_map/mul | solution.py:125
  19.8 0.6 collective-permute-done.3
  20.4 3.4 %pad_maximum_fusion.1 = (f32[4,9,8,2049]{3,1,2,0:T(8,128)S(1)}, f32[4,9,8,2049]{3,1,2,0:T(8,128)S(1)}) fusion(f32[4,9,8,1]{3,1,2,0:T(8,128)S(1)} %collective-permute-done.2, f32[1,9,8,2048]{3,1,2,0:T(8,128)} %bitcast.55, f32[3,9,8,2048]{3,1,2,0:T(8,128)S(1)} %copy.21, f32[4,9,8,1]{3,1,2,0:T(8,128)} %collective-permute-done.3), kind=kLoop, calls=%fused_computation.4 | loop fusion | flops 2360448 | bytes 7082496 | tf_op jit(solution)/shard_map/concatenate | solution.py:31
  23.8 1.6 %fusion.20 = (f32[1,9,8,2048]{3,1,2,0:T(8,128)S(1)}, f32[1,9,8,2048]{3,1,2,0:T(8,128)S(1)}) fusion(f32[4,9,1,2048]{3,1,2,0:T(8,128)} %collective-permute-done.1, f32[1,9,8,2048]{3,1,2,0:T(8,128)S(1)} %bitcast.56, f32[3,9,8,2048]{3,1,2,0:T(8,128)S(1)} %copy.21, f32[4,9,1,2048]{3,1,2,0:T(8,128)} %collective-permute-done, ...), kind=kLoop, calls=%fused_computation.39 | loop fusion | flops 1769472 | bytes 4131072 | tf_op jit(solution)/shard_map/mul | solution.py:102
  25.5 2.2 %maximum_maximum_fusion = (f32[4,9,9,2048]{3,1,2,0:T(8,128)S(1)}, f32[4,9,9,2048]{3,1,2,0:T(8,128)S(1)}) fusion(f32[1,9,8,2048]{3,1,2,0:T(8,128)S(1)} %bitcast.57, f32[3,9,8,2048]{3,1,2,0:T(8,128)S(1)} %copy.21, f32[4,9,1,2048]{3,1,2,0:T(8,128)} %collective-permute-done.1, f32[4,9,1,2048]{3,1,2,0:T(8,128)} %collective-permute-done), kind=kLoop, calls=%fused_computation.1 | loop fusion | flops 2654208 | bytes 8257536 | tf_op jit(solution)/shard_map/concatenate | solution.py:31
  27.7 6.5 %fusion.7 = f32[3,9,8,2048]{3,1,2,0:T(8,128)S(1)} fusion(f32[4,9,8,2049]{3,1,2,0:T(8,128)S(1)} %get-tuple-element.24, f32[4,9,8,2049]{3,1,2,0:T(8,128)S(1)} %get-tuple-element.23, f32[4,9,9,2048]{3,1,2,0:T(8,128)S(1)} %get-tuple-element.18, f32[1,9,8,2048]{3,1,2,0:T(8,128)S(1)} %get-tuple-element.20, f32[1,9,8,2048]{3,1,2,0:T(8,128)S(1)} %get-tuple-element.19, ...), kind=kOutput, calls=%fused_computation.14 | convolution fusion | flops 54855416 | bytes 20062720 | tf_op jit(solution)/shard_map/nm,cmar->cnar/dot_general | solution.py:96
  34.3 0.1 fusion.92
  34.4 2.3 %collective-permute-start.4 = (f32[1,9,1,2048]{3,1,2,0:T(8,128)S(1)}, f32[1,9,1,2048]{3,1,2,0:T(8,128)S(1)}, u32[]{:S(2)}, u32[]{:S(2)}) collective-permute-start(f32[1,9,1,2048]{3,1,2,0:T(8,128)S(1)} %get-tuple-element.27), channel_id=1, source_target_pairs={{4,0},{8,4},{12,8},{16,12},{20,16},{24,20},{28,24},{0,28},{5,1},{9... | collective-permute-start | bytes 221192 | tf_op jit(solution)/shard_map/ppermute | solution.py:30
  36.7 1.3 %collective-permute-start.6 = (f32[1,9,8,1]{3,1,2,0:T(8,128)S(1)}, f32[1,9,8,1]{3,1,2,0:T(8,128)S(1)}, u32[]{:S(2)}, u32[]{:S(2)}) collective-permute-start(f32[1,9,8,1]{3,1,2,0:T(8,128)S(1)} %get-tuple-element.31), channel_id=1, source_target_pairs={{1,0},{2,1},{3,2},{5,4},{6,5},{7,6},{9,8},{10,9},{11,10},{13,12},{... | collective-permute-start | bytes 872 | tf_op jit(solution)/shard_map/ppermute | solution.py:30
  38.0 4.7 %collective-permute-start.7 = (f32[1,9,8,1]{3,1,2,0:T(8,128)S(1)}, f32[1,9,8,1]{3,1,2,0:T(8,128)S(1)}, u32[]{:S(2)}, u32[]{:S(2)}) collective-permute-start(f32[1,9,8,1]{3,1,2,0:T(8,128)S(1)} %get-tuple-element.32), channel_id=1, source_target_pairs={{0,1},{1,2},{2,3},{4,5},{5,6},{6,7},{8,9},{9,10},{10,11},{12,13},{... | collective-permute-start | bytes 872 | tf_op jit(solution)/shard_map/ppermute | solution.py:27
  42.7 0.2 fusion.91
  43.0 1.6 %collective-permute-done.7 = f32[1,9,8,1]{3,1,2,0:T(8,128)S(1)} collective-permute-done((f32[1,9,8,1]{3,1,2,0:T(8,128)S(1)}, f32[1,9,8,1]{3,1,2,0:T(8,128)S(1)}, u32[]{:S(2)}, u32[]{:S(2)}) %collective-permute-start.7) | collective-permute-done | bytes 320 | tf_op jit(solution)/shard_map/ppermute | solution.py:27
  44.6 1.6 %broadcast_multiply_fusion = (f32[1,9,8,2048]{3,1,2,0:T(8,128)S(1)}, f32[1,9,8,2048]{3,1,2,0:T(8,128)}) fusion(f32[2048]{0:T(1024)S(1)} %copy-done.14, f32[1,9,8,2048]{3,1,2,0:T(8,128)S(1)} %get-tuple-element.30, f32[1,9,8,1]{3,1,2,0:T(8,128)S(1)} %collective-permute-done.7, f32[1,9,8,1]{3,1,2,0:T(8,128)S(1)} %collective-permute-done.6, ...), kind=kLoop, calls=%fused_computation.47 | loop fusion | flops 1327104 | bytes 2515520 | tf_op jit(solution)/shard_map/mul | solution.py:116
  46.3 0.8 fusion.93
  47.0 1.8 %collective-permute-start.8 = (f32[1,9,1,2048]{3,1,2,0:T(8,128)}, f32[1,9,1,2048]{3,1,2,0:T(8,128)S(1)}, u32[]{:S(2)}, u32[]{:S(2)}) collective-permute-start(f32[1,9,1,2048]{3,1,2,0:T(8,128)} %get-tuple-element.33), channel_id=1, source_target_pairs={{4,0},{8,4},{12,8},{16,12},{20,16},{24,20},{28,24},{0,28},{5,1},{9... | collective-permute-start | bytes 221192 | tf_op jit(solution)/shard_map/ppermute | solution.py:30
  48.8 0.7 fusion.94
  49.5 1.3 %collective-permute-start.10 = (f32[1,9,8,1]{3,1,2,0:T(8,128)}, f32[1,9,8,1]{3,1,2,0:T(8,128)}, u32[]{:S(2)}, u32[]{:S(2)}) collective-permute-start(f32[1,9,8,1]{3,1,2,0:T(8,128)} %get-tuple-element.35), channel_id=1, source_target_pairs={{1,0},{2,1},{3,2},{5,4},{6,5},{7,6},{9,8},{10,9},{11,10},{13,12},{... | collective-permute-start | bytes 872 | tf_op jit(solution)/shard_map/ppermute | solution.py:30
  50.8 5.2 %collective-permute-start.11 = (f32[1,9,8,1]{3,1,2,0:T(8,128)}, f32[1,9,8,1]{3,1,2,0:T(8,128)}, u32[]{:S(2)}, u32[]{:S(2)}) collective-permute-start(f32[1,9,8,1]{3,1,2,0:T(8,128)} %get-tuple-element.36), channel_id=1, source_target_pairs={{0,1},{1,2},{2,3},{4,5},{5,6},{6,7},{8,9},{9,10},{10,11},{12,13},{... | collective-permute-start | bytes 872 | tf_op jit(solution)/shard_map/ppermute | solution.py:27
  56.0 1.0 reshape.81
  57.0 1.0 reshape.82
  58.0 2.2 %copy.26 = f32[3,9,8,2048]{3,2,1,0:T(8,128)} copy(f32[3,9,8,2048]{3,1,2,0:T(8,128)S(1)} %fusion.7) | data formatting | bytes 3538944
  60.3 1.5 %fusion.12 = f32[1,9,8,2048]{3,1,2,0:T(8,128)S(1)} fusion(f32[1,9,8,2048]{3,1,2,0:T(8,128)S(1)} %copy-done.3, f32[1,9,8,2048]{3,1,2,0:T(8,128)S(1)} %copy-done.6, f32[1,9,8,1]{3,1,2,0:T(8,128)} %collective-permute-done.11, f32[1,9,8,1]{3,1,2,0:T(8,128)} %collective-permute-done.10, f32[1,9,1,2048]{3,1,2,0:T(8,128)S(1)} %collective-permute-done.9, ...), kind=kLoop, calls=%fused_computation.22 | loop fusion | flops 1916928 | bytes 1933888 | tf_op jit(solution)/shard_map/sub | solution.py:121
  61.9 0.3 copy.22
  62.2 3.7 %reshape_squeeze.3 = f32[9,2,4,128,16]{4,3,2,1,0:T(8,128)} reshape(f32[1,9,8,2048]{3,2,1,0:T(8,128)S(1)} %copy.22) | data formatting | bytes 1179648 | tf_op jit(solution)/shard_map/reshape;squeeze | solution.py:70
  66.0 3.9 %fusion.84 = (f32[9,2,128]{2,1,0:T(2,128)S(1)}, f32[9,2,128]{2,1,0:T(2,128)S(1)}, f32[9,2,128]{2,1,0:T(2,128)S(1)}) fusion(f32[9,2,4,128,16]{4,3,2,1,0:T(8,128)} %reshape_squeeze.3, f32[2,4,128,16]{3,2,1,0:T(8,128)S(1)} %copy-done.8, f32[2,4,128,16]{3,2,1,0:T(8,128)S(1)} %copy-done.7), kind=kLoop, calls=%fused_computation.140 | loop fusion | flops 730368 | bytes 748544 | tf_op jit(solution)/shard_map/reduce_sum | solution.py:70
  69.9 0.1 slice.287
  70.0 0.1 fusion.83
  70.1 2.4 %collective-permute-start.12 = (f32[1,9,1,128]{3,2,1,0:T(1,128)S(1)}, f32[1,9,1,128]{3,2,1,0:T(1,128)S(1)}, u32[]{:S(2)}, u32[]{:S(2)}) collective-permute-start(f32[1,9,1,128]{3,2,1,0:T(1,128)S(1)} %get-tuple-element.49), channel_id=1, source_target_pairs={{4,0},{8,4},{12,8},{16,12},{20,16},{24,20},{28,24},{0,28},{5,1},{9... | collective-permute-start | bytes 13832 | tf_op jit(solution)/shard_map/ppermute | solution.py:30
  72.5 0.1 fusion.101
  72.6 1.3 %collective-permute-start.14 = (f32[1,9,2,1]{3,2,1,0:T(2,128)S(1)}, f32[1,9,2,1]{3,2,1,0:T(2,128)S(1)}, u32[]{:S(2)}, u32[]{:S(2)}) collective-permute-start(f32[1,9,2,1]{3,2,1,0:T(2,128)S(1)} %get-tuple-element.51), channel_id=1, source_target_pairs={{1,0},{2,1},{3,2},{5,4},{6,5},{7,6},{9,8},{10,9},{11,10},{13,12},{... | collective-permute-start | bytes 224 | tf_op jit(solution)/shard_map/ppermute | solution.py:30
  73.9 4.5 %collective-permute-start.15 = (f32[1,9,2,1]{3,2,1,0:T(2,128)S(1)}, f32[1,9,2,1]{3,2,1,0:T(2,128)S(1)}, u32[]{:S(2)}, u32[]{:S(2)}) collective-permute-start(f32[1,9,2,1]{3,2,1,0:T(2,128)S(1)} %get-tuple-element.52), channel_id=1, source_target_pairs={{0,1},{1,2},{2,3},{4,5},{5,6},{6,7},{8,9},{9,10},{10,11},{12,13},{... | collective-permute-start | bytes 224 | tf_op jit(solution)/shard_map/ppermute | solution.py:27
  78.4 1.3 %collective-permute-done.15 = f32[1,9,2,1]{3,2,1,0:T(2,128)S(1)} collective-permute-done((f32[1,9,2,1]{3,2,1,0:T(2,128)S(1)}, f32[1,9,2,1]{3,2,1,0:T(2,128)S(1)}, u32[]{:S(2)}, u32[]{:S(2)}) %collective-permute-start.15) | collective-permute-done | bytes 104 | tf_op jit(solution)/shard_map/ppermute | solution.py:27
  79.8 0.1 divide_add_fusion.2
  79.9 1.6 %collective-permute-start.16 = (f32[1,9,1,128]{3,2,1,0:T(1,128)S(1)}, f32[1,9,1,128]{3,2,1,0:T(1,128)S(1)}, u32[]{:S(2)}, u32[]{:S(2)}) collective-permute-start(f32[1,9,1,128]{3,2,1,0:T(1,128)S(1)} %get-tuple-element.45), channel_id=1, source_target_pairs={{4,0},{8,4},{12,8},{16,12},{20,16},{24,20},{28,24},{0,28},{5,1},{9... | collective-permute-start | bytes 13832 | tf_op jit(solution)/shard_map/ppermute | solution.py:30
  81.5 0.1 fusion.99
  81.5 1.3 %collective-permute-start.18 = (f32[1,9,2,1]{3,2,1,0:T(2,128)S(1)}, f32[1,9,2,1]{3,2,1,0:T(2,128)S(1)}, u32[]{:S(2)}, u32[]{:S(2)}) collective-permute-start(f32[1,9,2,1]{3,2,1,0:T(2,128)S(1)} %get-tuple-element.47), channel_id=1, source_target_pairs={{1,0},{2,1},{3,2},{5,4},{6,5},{7,6},{9,8},{10,9},{11,10},{13,12},{... | collective-permute-start | bytes 224 | tf_op jit(solution)/shard_map/ppermute | solution.py:30
  82.8 4.5 %collective-permute-start.19 = (f32[1,9,2,1]{3,2,1,0:T(2,128)S(1)}, f32[1,9,2,1]{3,2,1,0:T(2,128)S(1)}, u32[]{:S(2)}, u32[]{:S(2)}) collective-permute-start(f32[1,9,2,1]{3,2,1,0:T(2,128)S(1)} %get-tuple-element.48), channel_id=1, source_target_pairs={{0,1},{1,2},{2,3},{4,5},{5,6},{6,7},{8,9},{9,10},{10,11},{12,13},{... | collective-permute-start | bytes 224 | tf_op jit(solution)/shard_map/ppermute | solution.py:27
  87.4 1.3 %collective-permute-done.19 = f32[1,9,2,1]{3,2,1,0:T(2,128)S(1)} collective-permute-done((f32[1,9,2,1]{3,2,1,0:T(2,128)S(1)}, f32[1,9,2,1]{3,2,1,0:T(2,128)S(1)}, u32[]{:S(2)}, u32[]{:S(2)}) %collective-permute-start.19) | collective-permute-done | bytes 104 | tf_op jit(solution)/shard_map/ppermute | solution.py:27
  88.8 0.1 divide_add_fusion.1
  88.9 1.8 %collective-permute-start.20 = (f32[1,9,1,128]{3,2,1,0:T(1,128)S(1)}, f32[1,9,1,128]{3,2,1,0:T(1,128)S(1)}, u32[]{:S(2)}, u32[]{:S(2)}) collective-permute-start(f32[1,9,1,128]{3,2,1,0:T(1,128)S(1)} %get-tuple-element.41), channel_id=1, source_target_pairs={{4,0},{8,4},{12,8},{16,12},{20,16},{24,20},{28,24},{0,28},{5,1},{9... | collective-permute-start | bytes 13832 | tf_op jit(solution)/shard_map/ppermute | solution.py:30
  90.7 0.1 fusion.97
  90.8 1.3 %collective-permute-start.22 = (f32[1,9,2,1]{3,2,1,0:T(2,128)S(1)}, f32[1,9,2,1]{3,2,1,0:T(2,128)S(1)}, u32[]{:S(2)}, u32[]{:S(2)}) collective-permute-start(f32[1,9,2,1]{3,2,1,0:T(2,128)S(1)} %get-tuple-element.43), channel_id=1, source_target_pairs={{1,0},{2,1},{3,2},{5,4},{6,5},{7,6},{9,8},{10,9},{11,10},{13,12},{... | collective-permute-start | bytes 224 | tf_op jit(solution)/shard_map/ppermute | solution.py:30
  92.1 4.8 %collective-permute-start.23 = (f32[1,9,2,1]{3,2,1,0:T(2,128)S(1)}, f32[1,9,2,1]{3,2,1,0:T(2,128)S(1)}, u32[]{:S(2)}, u32[]{:S(2)}) collective-permute-start(f32[1,9,2,1]{3,2,1,0:T(2,128)S(1)} %get-tuple-element.44), channel_id=1, source_target_pairs={{0,1},{1,2},{2,3},{4,5},{5,6},{6,7},{8,9},{9,10},{10,11},{12,13},{... | collective-permute-start | bytes 224 | tf_op jit(solution)/shard_map/ppermute | solution.py:27
  96.9 1.1 collective-permute-done.23
  98.0 0.1 divide_add_fusion
  98.1 0.1 fusion.95
  98.2 0.1 concatenate.126
  98.3 2.8 %broadcast_in_dim.31 = f32[9,2,4,128,16]{4,3,2,1,0:T(8,128)} broadcast(f32[9,2,128]{2,1,0:T(2,128)S(1)} %concatenate.126), dimensions={0,1,3} | broadcast | bytes 599040 | tf_op jit(solution)/shard_map/broadcast_in_dim | solution.py:85
  101.1 5.0 %reshape.78 = f32[9,8,2048]{2,1,0:T(8,128)S(1)} reshape(f32[9,2,4,128,16]{4,3,2,1,0:T(8,128)} %broadcast_in_dim.31) | data formatting | bytes 1179648 | tf_op jit(solution)/shard_map/reshape | solution.py:86
  106.1 2.8 %broadcast_in_dim.33 = f32[9,2,4,128,16]{4,3,2,1,0:T(8,128)} broadcast(f32[9,2,128]{2,1,0:T(2,128)S(1)} %concatenate.127), dimensions={0,1,3} | broadcast | bytes 599040 | tf_op jit(solution)/shard_map/broadcast_in_dim | solution.py:85
  108.9 5.0 %reshape.79 = f32[9,8,2048]{2,1,0:T(8,128)S(1)} reshape(f32[9,2,4,128,16]{4,3,2,1,0:T(8,128)} %broadcast_in_dim.33) | data formatting | bytes 1179648 | tf_op jit(solution)/shard_map/reshape | solution.py:86
  113.9 2.8 %broadcast_in_dim.34 = f32[9,2,4,128,16]{4,3,2,1,0:T(8,128)} broadcast(f32[9,2,128]{2,1,0:T(2,128)S(1)} %divide_add_fusion), dimensions={0,1,3} | broadcast | bytes 599040 | tf_op jit(solution)/shard_map/broadcast_in_dim | solution.py:85
  116.7 5.1 %reshape.80 = f32[9,8,2048]{2,1,0:T(8,128)S(1)} reshape(f32[9,2,4,128,16]{4,3,2,1,0:T(8,128)} %broadcast_in_dim.34) | data formatting | bytes 1179648 | tf_op jit(solution)/shard_map/reshape | solution.py:86
  121.8 1.1 fusion.21
  123.0 1.2 copy.27
  (67 shorter events, 0.3 us)
Async XLA Ops:
  0.6 2.7 %copy-start.9 = (f32[9,8,2048]{2,1,0:T(8,128)S(1)}, f32[9,8,2048]{2,1,0:T(8,128)}, u32[]{:S(2)}) copy-start(f32[9,8,2048]{2,1,0:T(8,128)} %param.7) | copy-start | bytes 1769476
  3.7 5.4 %copy-start = (f32[9,8,2048]{2,0,1:T(8,128)}, f32[9,8,2048]{2,0,1:T(8,128)S(1)}, u32[]{:S(2)}) copy-start(f32[9,8,2048]{2,0,1:T(8,128)S(1)} %copy.39) | copy-start | bytes 1769476
  4.9 12.0 %copy-start.13 = (f32[8,2048]{1,0:T(8,128)S(1)}, f32[8,2048]{1,0:T(8,128)}, u32[]{:S(2)}) copy-start(f32[8,2048]{1,0:T(8,128)} %param.8) | copy-start | bytes 196612
  4.9 18.9 %collective-permute-start = (f32[4,9,1,2048]{3,1,2,0:T(8,128)}, f32[4,9,1,2048]{3,1,2,0:T(8,128)}, u32[]{:S(2)}, u32[]{:S(2)}) collective-permute-start(f32[4,9,1,2048]{3,1,2,0:T(8,128)} %get-tuple-element.22), channel_id=1, source_target_pairs={{4,0},{8,4},{12,8},{16,12},{20,16},{24,20},{28,24},{0,28},{5,1},{9... | collective-permute-start | bytes 884744 | tf_op jit(solution)/shard_map/ppermute | solution.py:30
  8.2 15.6 %collective-permute-start.1 = (f32[4,9,1,2048]{3,1,2,0:T(8,128)}, f32[4,9,1,2048]{3,1,2,0:T(8,128)}, u32[]{:S(2)}, u32[]{:S(2)}) collective-permute-start(f32[4,9,1,2048]{3,1,2,0:T(8,128)} %get-tuple-element.21), channel_id=1, source_target_pairs={{0,4},{4,8},{8,12},{12,16},{16,20},{20,24},{24,28},{28,0},{1,5},{5... | collective-permute-start | bytes 884744 | tf_op jit(solution)/shard_map/ppermute | solution.py:27
  9.1 10.7 %collective-permute-start.2 = (f32[4,9,8,1]{3,1,2,0:T(8,128)}, f32[4,9,8,1]{3,1,2,0:T(8,128)S(1)}, u32[]{:S(2)}, u32[]{:S(2)}) collective-permute-start(f32[4,9,8,1]{3,1,2,0:T(8,128)} %get-tuple-element.25), channel_id=1, source_target_pairs={{1,0},{2,1},{3,2},{5,4},{6,5},{7,6},{9,8},{10,9},{11,10},{13,12},{... | collective-permute-start | bytes 3464 | tf_op jit(solution)/shard_map/ppermute | solution.py:30
  10.4 10.0 %collective-permute-start.3 = (f32[4,9,8,1]{3,1,2,0:T(8,128)}, f32[4,9,8,1]{3,1,2,0:T(8,128)}, u32[]{:S(2)}, u32[]{:S(2)}) collective-permute-start(f32[4,9,8,1]{3,1,2,0:T(8,128)} %get-tuple-element.26), channel_id=1, source_target_pairs={{0,1},{1,2},{2,3},{4,5},{5,6},{6,7},{8,9},{9,10},{10,11},{12,13},{... | collective-permute-start | bytes 3464 | tf_op jit(solution)/shard_map/ppermute | solution.py:27
  19.8 4.1 %copy-start.1 = (f32[9,8,2048]{2,0,1:T(8,128)S(1)}, f32[9,8,2048]{2,0,1:T(8,128)}, u32[]{:S(2)}) copy-start(f32[9,8,2048]{2,0,1:T(8,128)} %copy-done) | copy-start | bytes 1769476
  25.5 2.2 %copy-start.2 = (f32[3,9,8,2048]{3,2,1,0:T(8,128)S(1)}, f32[3,9,8,2048]{3,2,1,0:T(8,128)}, u32[]{:S(2)}) copy-start(f32[3,9,8,2048]{3,2,1,0:T(8,128)} %param.6) | copy-start | bytes 5308420
  34.2 10.4 %copy-start.14 = (f32[2048]{0:T(1024)S(1)}, f32[2048]{0:T(1024)}, u32[]{:S(2)}) copy-start(f32[2048]{0:T(1024)} %fusion.61) | copy-start | bytes 24580
  34.4 10.3 %collective-permute-start.4 = (f32[1,9,1,2048]{3,1,2,0:T(8,128)S(1)}, f32[1,9,1,2048]{3,1,2,0:T(8,128)S(1)}, u32[]{:S(2)}, u32[]{:S(2)}) collective-permute-start(f32[1,9,1,2048]{3,1,2,0:T(8,128)S(1)} %get-tuple-element.27), channel_id=1, source_target_pairs={{4,0},{8,4},{12,8},{16,12},{20,16},{24,20},{28,24},{0,28},{5,1},{9... | collective-permute-start | bytes 221192 | tf_op jit(solution)/shard_map/ppermute | solution.py:30
  36.7 7.9 %collective-permute-start.5 = (f32[1,9,1,2048]{3,1,2,0:T(8,128)S(1)}, f32[1,9,1,2048]{3,1,2,0:T(8,128)S(1)}, u32[]{:S(2)}, u32[]{:S(2)}) collective-permute-start(f32[1,9,1,2048]{3,1,2,0:T(8,128)S(1)} %get-tuple-element.28), channel_id=1, source_target_pairs={{0,4},{4,8},{8,12},{12,16},{16,20},{20,24},{24,28},{28,0},{1,5},{5... | collective-permute-start | bytes 221192 | tf_op jit(solution)/shard_map/ppermute | solution.py:27
  36.7 6.3 %collective-permute-start.6 = (f32[1,9,8,1]{3,1,2,0:T(8,128)S(1)}, f32[1,9,8,1]{3,1,2,0:T(8,128)S(1)}, u32[]{:S(2)}, u32[]{:S(2)}) collective-permute-start(f32[1,9,8,1]{3,1,2,0:T(8,128)S(1)} %get-tuple-element.31), channel_id=1, source_target_pairs={{1,0},{2,1},{3,2},{5,4},{6,5},{7,6},{9,8},{10,9},{11,10},{13,12},{... | collective-permute-start | bytes 872 | tf_op jit(solution)/shard_map/ppermute | solution.py:30
  38.0 6.6 %collective-permute-start.7 = (f32[1,9,8,1]{3,1,2,0:T(8,128)S(1)}, f32[1,9,8,1]{3,1,2,0:T(8,128)S(1)}, u32[]{:S(2)}, u32[]{:S(2)}) collective-permute-start(f32[1,9,8,1]{3,1,2,0:T(8,128)S(1)} %get-tuple-element.32), channel_id=1, source_target_pairs={{0,1},{1,2},{2,3},{4,5},{5,6},{6,7},{8,9},{9,10},{10,11},{12,13},{... | collective-permute-start | bytes 872 | tf_op jit(solution)/shard_map/ppermute | solution.py:27
  42.9 13.1 %copy-start.10 = (f32[8,2048]{1,0:T(8,128)S(1)}, f32[8,2048]{1,0:T(8,128)}, u32[]{:S(2)}) copy-start(f32[8,2048]{1,0:T(8,128)} %get-tuple-element.11) | copy-start | bytes 196612
  46.3 2.6 %copy-start.5 = (f32[1,9,8,2048]{3,1,2,0:T(8,128)}, f32[1,9,8,2048]{3,1,2,0:T(8,128)S(1)}, u32[]{:S(2)}) copy-start(f32[1,9,8,2048]{3,1,2,0:T(8,128)S(1)} %get-tuple-element.15) | copy-start | bytes 1769476
  47.0 13.3 %collective-permute-start.8 = (f32[1,9,1,2048]{3,1,2,0:T(8,128)}, f32[1,9,1,2048]{3,1,2,0:T(8,128)S(1)}, u32[]{:S(2)}, u32[]{:S(2)}) collective-permute-start(f32[1,9,1,2048]{3,1,2,0:T(8,128)} %get-tuple-element.33), channel_id=1, source_target_pairs={{4,0},{8,4},{12,8},{16,12},{20,16},{24,20},{28,24},{0,28},{5,1},{9... | collective-permute-start | bytes 221192 | tf_op jit(solution)/shard_map/ppermute | solution.py:30
  48.8 11.5 %collective-permute-start.9 = (f32[1,9,1,2048]{3,1,2,0:T(8,128)}, f32[1,9,1,2048]{3,1,2,0:T(8,128)S(1)}, u32[]{:S(2)}, u32[]{:S(2)}) collective-permute-start(f32[1,9,1,2048]{3,1,2,0:T(8,128)} %get-tuple-element.34), channel_id=1, source_target_pairs={{0,4},{4,8},{8,12},{12,16},{16,20},{20,24},{24,28},{28,0},{1,5},{5... | collective-permute-start | bytes 221192 | tf_op jit(solution)/shard_map/ppermute | solution.py:27
  49.5 10.8 %collective-permute-start.10 = (f32[1,9,8,1]{3,1,2,0:T(8,128)}, f32[1,9,8,1]{3,1,2,0:T(8,128)}, u32[]{:S(2)}, u32[]{:S(2)}) collective-permute-start(f32[1,9,8,1]{3,1,2,0:T(8,128)} %get-tuple-element.35), channel_id=1, source_target_pairs={{1,0},{2,1},{3,2},{5,4},{6,5},{7,6},{9,8},{10,9},{11,10},{13,12},{... | collective-permute-start | bytes 872 | tf_op jit(solution)/shard_map/ppermute | solution.py:30
  50.8 9.5 %collective-permute-start.11 = (f32[1,9,8,1]{3,1,2,0:T(8,128)}, f32[1,9,8,1]{3,1,2,0:T(8,128)}, u32[]{:S(2)}, u32[]{:S(2)}) collective-permute-start(f32[1,9,8,1]{3,1,2,0:T(8,128)} %get-tuple-element.36), channel_id=1, source_target_pairs={{0,1},{1,2},{2,3},{4,5},{5,6},{6,7},{8,9},{9,10},{10,11},{12,13},{... | collective-permute-start | bytes 872 | tf_op jit(solution)/shard_map/ppermute | solution.py:27
  58.0 2.3 %copy-start.3 = (f32[1,9,8,2048]{3,1,2,0:T(8,128)S(1)}, f32[1,9,8,2048]{3,1,2,0:T(8,128)}, u32[]{:S(2)}) copy-start(f32[1,9,8,2048]{3,1,2,0:T(8,128)} %get-tuple-element.16) | copy-start | bytes 1769476
  58.0 2.3 %copy-start.6 = (f32[1,9,8,2048]{3,1,2,0:T(8,128)S(1)}, f32[1,9,8,2048]{3,1,2,0:T(8,128)}, u32[]{:S(2)}) copy-start(f32[1,9,8,2048]{3,1,2,0:T(8,128)} %copy-done.5) | copy-start | bytes 1769476
  61.8 4.1 %copy-start.7 = (f32[2,4,128,16]{3,2,1,0:T(8,128)S(1)}, f32[2,4,128,16]{3,2,1,0:T(8,128)}, u32[]{:S(2)}) copy-start(f32[2,4,128,16]{3,2,1,0:T(8,128)} %reshape.81) | copy-start | bytes 196612
  61.9 4.1 %copy-start.8 = (f32[2,4,128,16]{3,2,1,0:T(8,128)S(1)}, f32[2,4,128,16]{3,2,1,0:T(8,128)}, u32[]{:S(2)}) copy-start(f32[2,4,128,16]{3,2,1,0:T(8,128)} %reshape.82) | copy-start | bytes 196612
  66.0 4.0 %copy-start.15 = (f32[2,128]{1,0:T(2,128)S(1)}, f32[2,128]{1,0:T(2,128)}, u32[]{:S(2)}) copy-start(f32[2,128]{1,0:T(2,128)} %broadcast_add_fusion) | copy-start | bytes 3076
  70.1 9.7 %collective-permute-start.12 = (f32[1,9,1,128]{3,2,1,0:T(1,128)S(1)}, f32[1,9,1,128]{3,2,1,0:T(1,128)S(1)}, u32[]{:S(2)}, u32[]{:S(2)}) collective-permute-start(f32[1,9,1,128]{3,2,1,0:T(1,128)S(1)} %get-tuple-element.49), channel_id=1, source_target_pairs={{4,0},{8,4},{12,8},{16,12},{20,16},{24,20},{28,24},{0,28},{5,1},{9... | collective-permute-start | bytes 13832 | tf_op jit(solution)/shard_map/ppermute | solution.py:30
  72.5 7.3 %collective-permute-start.13 = (f32[1,9,1,128]{3,2,1,0:T(1,128)S(1)}, f32[1,9,1,128]{3,2,1,0:T(1,128)S(1)}, u32[]{:S(2)}, u32[]{:S(2)}) collective-permute-start(f32[1,9,1,128]{3,2,1,0:T(1,128)S(1)} %get-tuple-element.50), channel_id=1, source_target_pairs={{0,4},{4,8},{8,12},{12,16},{16,20},{20,24},{24,28},{28,0},{1,5},{5... | collective-permute-start | bytes 13832 | tf_op jit(solution)/shard_map/ppermute | solution.py:27
  72.6 5.9 %collective-permute-start.14 = (f32[1,9,2,1]{3,2,1,0:T(2,128)S(1)}, f32[1,9,2,1]{3,2,1,0:T(2,128)S(1)}, u32[]{:S(2)}, u32[]{:S(2)}) collective-permute-start(f32[1,9,2,1]{3,2,1,0:T(2,128)S(1)} %get-tuple-element.51), channel_id=1, source_target_pairs={{1,0},{2,1},{3,2},{5,4},{6,5},{7,6},{9,8},{10,9},{11,10},{13,12},{... | collective-permute-start | bytes 224 | tf_op jit(solution)/shard_map/ppermute | solution.py:30
  73.9 5.9 %collective-permute-start.15 = (f32[1,9,2,1]{3,2,1,0:T(2,128)S(1)}, f32[1,9,2,1]{3,2,1,0:T(2,128)S(1)}, u32[]{:S(2)}, u32[]{:S(2)}) collective-permute-start(f32[1,9,2,1]{3,2,1,0:T(2,128)S(1)} %get-tuple-element.52), channel_id=1, source_target_pairs={{0,1},{1,2},{2,3},{4,5},{5,6},{6,7},{8,9},{9,10},{10,11},{12,13},{... | collective-permute-start | bytes 224 | tf_op jit(solution)/shard_map/ppermute | solution.py:27
  79.9 8.8 %collective-permute-start.16 = (f32[1,9,1,128]{3,2,1,0:T(1,128)S(1)}, f32[1,9,1,128]{3,2,1,0:T(1,128)S(1)}, u32[]{:S(2)}, u32[]{:S(2)}) collective-permute-start(f32[1,9,1,128]{3,2,1,0:T(1,128)S(1)} %get-tuple-element.45), channel_id=1, source_target_pairs={{4,0},{8,4},{12,8},{16,12},{20,16},{24,20},{28,24},{0,28},{5,1},{9... | collective-permute-start | bytes 13832 | tf_op jit(solution)/shard_map/ppermute | solution.py:30
  81.5 7.3 %collective-permute-start.17 = (f32[1,9,1,128]{3,2,1,0:T(1,128)S(1)}, f32[1,9,1,128]{3,2,1,0:T(1,128)S(1)}, u32[]{:S(2)}, u32[]{:S(2)}) collective-permute-start(f32[1,9,1,128]{3,2,1,0:T(1,128)S(1)} %get-tuple-element.46), channel_id=1, source_target_pairs={{0,4},{4,8},{8,12},{12,16},{16,20},{20,24},{24,28},{28,0},{1,5},{5... | collective-permute-start | bytes 13832 | tf_op jit(solution)/shard_map/ppermute | solution.py:27
  81.5 5.9 %collective-permute-start.18 = (f32[1,9,2,1]{3,2,1,0:T(2,128)S(1)}, f32[1,9,2,1]{3,2,1,0:T(2,128)S(1)}, u32[]{:S(2)}, u32[]{:S(2)}) collective-permute-start(f32[1,9,2,1]{3,2,1,0:T(2,128)S(1)} %get-tuple-element.47), channel_id=1, source_target_pairs={{1,0},{2,1},{3,2},{5,4},{6,5},{7,6},{9,8},{10,9},{11,10},{13,12},{... | collective-permute-start | bytes 224 | tf_op jit(solution)/shard_map/ppermute | solution.py:30
  82.8 5.9 %collective-permute-start.19 = (f32[1,9,2,1]{3,2,1,0:T(2,128)S(1)}, f32[1,9,2,1]{3,2,1,0:T(2,128)S(1)}, u32[]{:S(2)}, u32[]{:S(2)}) collective-permute-start(f32[1,9,2,1]{3,2,1,0:T(2,128)S(1)} %get-tuple-element.48), channel_id=1, source_target_pairs={{0,1},{1,2},{2,3},{4,5},{5,6},{6,7},{8,9},{9,10},{10,11},{12,13},{... | collective-permute-start | bytes 224 | tf_op jit(solution)/shard_map/ppermute | solution.py:27
  88.9 9.1 %collective-permute-start.20 = (f32[1,9,1,128]{3,2,1,0:T(1,128)S(1)}, f32[1,9,1,128]{3,2,1,0:T(1,128)S(1)}, u32[]{:S(2)}, u32[]{:S(2)}) collective-permute-start(f32[1,9,1,128]{3,2,1,0:T(1,128)S(1)} %get-tuple-element.41), channel_id=1, source_target_pairs={{4,0},{8,4},{12,8},{16,12},{20,16},{24,20},{28,24},{0,28},{5,1},{9... | collective-permute-start | bytes 13832 | tf_op jit(solution)/shard_map/ppermute | solution.py:30
  90.7 7.3 %collective-permute-start.21 = (f32[1,9,1,128]{3,2,1,0:T(1,128)S(1)}, f32[1,9,1,128]{3,2,1,0:T(1,128)S(1)}, u32[]{:S(2)}, u32[]{:S(2)}) collective-permute-start(f32[1,9,1,128]{3,2,1,0:T(1,128)S(1)} %get-tuple-element.42), channel_id=1, source_target_pairs={{0,4},{4,8},{8,12},{12,16},{16,20},{20,24},{24,28},{28,0},{1,5},{5... | collective-permute-start | bytes 13832 | tf_op jit(solution)/shard_map/ppermute | solution.py:27
  90.8 6.1 %collective-permute-start.22 = (f32[1,9,2,1]{3,2,1,0:T(2,128)S(1)}, f32[1,9,2,1]{3,2,1,0:T(2,128)S(1)}, u32[]{:S(2)}, u32[]{:S(2)}) collective-permute-start(f32[1,9,2,1]{3,2,1,0:T(2,128)S(1)} %get-tuple-element.43), channel_id=1, source_target_pairs={{1,0},{2,1},{3,2},{5,4},{6,5},{7,6},{9,8},{10,9},{11,10},{13,12},{... | collective-permute-start | bytes 224 | tf_op jit(solution)/shard_map/ppermute | solution.py:30
  92.1 5.9 %collective-permute-start.23 = (f32[1,9,2,1]{3,2,1,0:T(2,128)S(1)}, f32[1,9,2,1]{3,2,1,0:T(2,128)S(1)}, u32[]{:S(2)}, u32[]{:S(2)}) collective-permute-start(f32[1,9,2,1]{3,2,1,0:T(2,128)S(1)} %get-tuple-element.44), channel_id=1, source_target_pairs={{0,1},{1,2},{2,3},{4,5},{5,6},{6,7},{8,9},{9,10},{10,11},{12,13},{... | collective-permute-start | bytes 224 | tf_op jit(solution)/shard_map/ppermute | solution.py:27
  116.7 5.1 %copy-start.4 = (f32[1,9,8,2048]{3,1,2,0:T(8,128)S(1)}, f32[1,9,8,2048]{3,1,2,0:T(8,128)}, u32[]{:S(2)}) copy-start(f32[1,9,8,2048]{3,1,2,0:T(8,128)} %get-tuple-element.16) | copy-start | bytes 1769476
  116.7 5.1 %copy-start.11 = (pred[8,2048]{1,0:T(8,128)(4,1)S(1)}, pred[8,2048]{1,0:T(8,128)(4,1)}, u32[]{:S(2)}) copy-start(pred[8,2048]{1,0:T(8,128)(4,1)} %get-tuple-element.12) | copy-start | bytes 49156
  116.7 5.1 %copy-start.12 = (pred[8,2048]{1,0:T(8,128)(4,1)S(1)}, pred[8,2048]{1,0:T(8,128)(4,1)}, u32[]{:S(2)}) copy-start(pred[8,2048]{1,0:T(8,128)(4,1)} %get-tuple-element.38) | copy-start | bytes 49156
where the time goes:
time: 125 us; the launch traced here: 124 us
  starting transfers between devices  50 us (40%)
  local copies, waits for them, and re-layouts  38.4 us (31%)
  other arithmetic  21.3 us (17%)
  matrix products  6.55 us (5%)
  waiting for transfers between devices  6.14 us (5%)
  between operations  1.76 us (1%)
    ppermute x12, starting transfers between devices, padded(): lax.ppermute(lax.slice_in_dim(block, block.shape[dim] - width, None, axis...  29.1 us
    ppermute x12, starting transfers between devices, padded(): lax.ppermute(lax.slice_in_dim(block, 0, width, axis=dim), axis, backward)  20.9 us
    reshape x3, local copies, waits for them, and re-layouts, expand(): return wide.reshape(ntime, planes, cells)  15 us
    broadcast_in_dim x3, local copies, waits for them, and re-layouts, expand(): jnp.broadcast_to(field[:, :, None, :, None], (ntime, cplanes, 4, ccells,...  8.43 us
    dot_general x1, matrix products, shards(): jnp.einsum('nm,cmar->cnar', coupling, velocity, precision=lax.Precision.H...  6.55 us
    unnamed x36, local copies, waits for them, and re-layouts  6.47 us
    ppermute x12, waiting for transfers between devices, padded(): lax.ppermute(lax.slice_in_dim(block, block.shape[dim] - width, None, axis...  6.05 us
    concatenate x2, other arithmetic, padded(): block = jnp.concatenate([low, block, high], axis=dim)  5.56 us
  transfers between devices with their start and end apart: 24, of which 6 were waited for; matrix products, arithmetic and copies ran while one was open for 11% of the time, Pallas kernels for 0%

commit v1 on v0

v1 whole, which is shorter than its diff:
```python
import functools
import math

import jax
import jax.numpy as jnp
import numpy as np
from jax import lax
from jax.experimental import pallas as pl
from jax.experimental.pallas import tpu as pltpu
from jax.sharding import PartitionSpec as P

MESH = pl.DeviceIdType.MESH
BLOCKS = 8
CSWEEPS = 4
NT = 9
FAN = 16
F32 = jnp.float32
BF16 = jnp.bfloat16

DIRS = [(1, 0), (-1, 0), (2, 0), (-2, 0)] + [
    (dt, ds) for ds in (1, -1) for dt in (0, 1, -1, 2, -2)
]
DIAG = [(1, 1), (1, -1), (-1, 1), (-1, -1)]
FREQ = [0.15 * (-1.0) ** d / math.sin(math.pi * d / NT) for d in range(1, 5)]


def kernel(
    n_theta, n_span,
    live_ref, v_ref, p_ref, d_ref, own_ref, cd_ref,
    pred_ref, corr_ref,
    tsend, trecv, ssend, srecv, dsend, drecv, bsend, brecv,
    sm_ref, stay, moved, st1, st2, edge0, lhs,
    send_sem, recv_sem,
):
    cells = v_ref.shape[1]
    cols = cells // FAN
    t, s = lax.axis_index("theta"), lax.axis_index("span")
    tile = lambda i: pl.ds(pl.multiple_of(i * 8, 8), 8)

    def peer(dt, ds):
        return (lax.rem(t + dt + n_theta, n_theta), s + ds)

    def there(ds, act):
        if ds == 0:
            act()
        elif ds > 0:
            pl.when(s < n_span - 1)(act)
        else:
            pl.when(s > 0)(act)

    def remote(src, dst, slot, dt, ds):
        return pltpu.make_async_remote_copy(
            src_ref=src, dst_ref=dst, send_sem=send_sem.at[slot], recv_sem=recv_sem.at[slot],
            device_id=peer(dt, ds), device_id_type=MESH)

    barrier = pltpu.get_barrier_semaphore()
    for dt, ds in DIRS:
        there(ds, lambda dt=dt, ds=ds: pl.semaphore_signal(
            barrier, inc=1, device_id=peer(dt, ds), device_id_type=MESH))

    lane = lax.broadcasted_iota(jnp.int32, (1, cells), 1)
    row8 = lax.broadcasted_iota(jnp.int32, (8, 1), 0)
    lane128 = lax.broadcasted_iota(jnp.int32, (8, 128), 1)
    row128 = lax.broadcasted_iota(jnp.int32, (8, 128), 0)
    live = live_ref[0, 0]
    fl = (lane < live * (cells // BLOCKS)).astype(F32)
    base = s * cols + lane // FAN
    mv = (own_ref[...] != base).astype(F32)
    df = d_ref[...] * (0.1 * fl)

    def pack(way, row, ref, plane, count):
        for i in range(count):
            tsend[way, row + i:row + i + 1, :] = ref[8 * i + plane:8 * i + plane + 1, :]

    for way, plane in ((0, 7), (1, 0)):
        pack(way, 0, v_ref, plane, 27)
        pack(way, 27, p_ref, plane, 9)
        tsend[way, 36:37, :] = df[plane:plane + 1, :]
        tsend[way, 37:38, :] = mv[plane:plane + 1, :]
        tsend[way, 38:39, :] = fl
    for i, (dt, ds) in enumerate(DIAG):
        way = 0 if dt > 0 else 1
        c0 = cells - 128 if ds > 0 else 0
        at = 127 if ds > 0 else 0
        a0 = tsend[way, 0:9, c0:c0 + 128][:, at:at + 1]
        a1 = tsend[way, 9:18, c0:c0 + 128][:, at:at + 1]
        l9 = lax.broadcasted_iota(jnp.int32, (9, 128), 1)
        dsend[i, 0:9, :] = jnp.where(l9 == 0, a0, a1)

    pl.semaphore_wait(barrier, jnp.where((s > 0) & (s < n_span - 1), 14, 9))

    m1 = [remote(tsend.at[w, 0:32], trecv.at[w, 0:32], w, 1 - 2 * w, 0) for w in range(2)]
    m2 = [remote(tsend.at[w, 32:48], trecv.at[w, 32:48], 2 + w, 1 - 2 * w, 0) for w in range(2)]
    ms = [remote(ssend.at[w], srecv.at[w], 4 + w, 0, 1 - 2 * w) for w in range(2)]
    md = [remote(dsend.at[i], drecv.at[i], 6 + i, dt, ds) for i, (dt, ds) in enumerate(DIAG)]
    mb = [remote(bsend, brecv.at[i], 10 + i, dt, ds) for i, (dt, ds) in enumerate(DIRS)]
    for m in m1:
        m.start()
    for m, (dt, ds) in zip(md, DIAG):
        there(ds, m.start)

    def clear(ds):
        w = 0 if ds < 0 else 1
        srecv[w] = jnp.zeros(srecv.shape[1:], F32)
        for i, (_, e) in enumerate(DIAG):
            if e == -ds:
                drecv[i] = jnp.zeros(drecv.shape[1:], F32)
        for i, (_, e) in enumerate(DIRS):
            if e == -ds:
                brecv[i] = jnp.zeros(brecv.shape[1:], F32)

    pl.when(s == 0)(lambda: clear(-1))
    pl.when(s == n_span - 1)(lambda: clear(1))

    def a_pair(x):
        return (jnp.where(row8 == 7, 0.0, pltpu.roll(x, 7, 0)),
                jnp.where(row8 == 0, 0.0, pltpu.roll(x, 1, 0)))

    def r_pair(x):
        return (jnp.where(lane == cells - 1, 0.0, pltpu.roll(x, cells - 1, 1)),
                jnp.where(lane == 0, 0.0, pltpu.roll(x, 1, 1)))

    width = 256
    for c in range(3):
        def source(j, _):
            at = pl.ds(pl.multiple_of(j * width, width), width)
            x = [v_ref[(c * NT + n) * 8:(c * NT + n) * 8 + 8, at] for n in range(NT)]
            acc = list(x)
            for d in range(1, 5):
                for n in range(NT):
                    gap = (x[(n - d) % NT] - x[(n + d) % NT]) * (0.2 * FREQ[d - 1])
                    acc[n] = acc[n] - gap
            for n in range(NT):
                pred_ref[(c * NT + n) * 8:(c * NT + n) * 8 + 8, at] = acc[n]
            return 0

        lax.fori_loop(0, cells // width, source, 0)

        def local(n, _):
            x = v_ref[tile(c * NT + n), :]
            ap, am = a_pair(x)
            rp, rm = r_pair(x)
            out = pred_ref[tile(c * NT + n), :] - 0.1 * (x - am)
            if c < 2:
                q = p_ref[tile(n), :]
                qp, qm = a_pair(q) if c == 0 else r_pair(q)
                out = out - 0.1 * (qp - qm)
            pred_ref[tile(c * NT + n), :] = fl * out + df * (ap + am + rp + rm - 4.0 * x)
            return 0

        lax.fori_loop(0, NT, local, 0)

        if c == 0:
            for way, plane in ((0, 7), (1, 0)):
                pack(way, 39, pred_ref, plane, 9)
                m2[way].start()
        if c == 1:
            def columns(n, _):
                for way in range(2):
                    c0, at = (cells - 128, 127) if way == 0 else (0, 0)
                    got = jnp.zeros((8, 128), F32)
                    for f, x in enumerate((
                        v_ref[tile(n), c0:c0 + 128], v_ref[tile(NT + n), c0:c0 + 128],
                        v_ref[tile(2 * NT + n), c0:c0 + 128], p_ref[tile(n), c0:c0 + 128],
                        pred_ref[tile(NT + n), c0:c0 + 128], df[:, c0:c0 + 128],
                        jnp.broadcast_to(fl[:, c0:c0 + 128], (8, 128)))):
                        got = jnp.where(lane128 == f, x[:, at:at + 1], got)
                    ssend[way, tile(n), :] = got
                return 0

            lax.fori_loop(0, NT, columns, 0)
            for m, ds in zip(ms, (1, -1)):
                there(ds, m.start)

    def members(j, _):
        at = pl.ds(pl.multiple_of(j * width, width), width)
        r = lax.broadcasted_iota(jnp.int32, (256, width), 1) + j * width
        k = lax.broadcasted_iota(jnp.int32, (256, width), 0) & 127
        b = r // FAN
        e = r % FAN
        to = jnp.where(e == 0, b - 1, jnp.where(e == FAN - 1, b + 1, -9))
        st1[:, at] = (b == k).astype(F32).astype(BF16)
        st2[:, at] = (to == k).astype(F32).astype(BF16)
        return 0

    lax.fori_loop(0, cells // width, members, 0)

    for m in m1 + m2:
        m.wait_recv()
    for m, (dt, ds) in zip(md, DIAG):
        there(-ds, m.wait_recv)
    for m, ds in zip(ms, (1, -1)):
        there(-ds, m.wait_recv)

    df_dn, fl_dn = trecv[0, 36:37, :], trecv[0, 38:39, :]
    df_up, fl_up = trecv[1, 36:37, :], trecv[1, 38:39, :]
    lo, hi = lane == 0, lane == cells - 1
    edge0[0] = (trecv[0, 39:48, :] + df_dn * tsend[1, 0:9, :] - 0.1 * fl_dn * tsend[1, 27:36, :]
                + jnp.where(lo, df_dn * drecv[0, 0:9, 0:1], 0.0)
                + jnp.where(hi, df_dn * drecv[1, 0:9, 0:1], 0.0))
    edge0[1] = (trecv[1, 39:48, :] + (df_up + 0.1 * fl_up) * tsend[0, 0:9, :]
                + 0.1 * fl_up * tsend[0, 27:36, :]
                + jnp.where(lo, df_up * drecv[2, 0:9, 0:1], 0.0)
                + jnp.where(hi, df_up * drecv[3, 0:9, 0:1], 0.0))
    w_dn = jnp.where(row8 == 0, df + 0.1 * fl, 0.0)
    w_up = jnp.where(row8 == 7, df, 0.0)
    q_dn = jnp.where(row8 == 0, 0.1 * fl, 0.0)
    q_up = jnp.where(row8 == 7, 0.1 * fl, 0.0)

    def complete(n, _):
        left, right = srecv[0, tile(n), :], srecv[1, tile(n), :]
        for c in range(3):
            i = c * NT + n
            out = (pred_ref[tile(i), :] + w_dn * trecv[0, pl.ds(i, 1), :]
                   + w_up * trecv[1, pl.ds(i, 1), :])
            a, b = df * left[:, c:c + 1], df * right[:, c:c + 1]
            if c == 0:
                out = (out + q_dn * trecv[0, pl.ds(27 + n, 1), :]
                       - q_up * trecv[1, pl.ds(27 + n, 1), :])
            if c == 1:
                a = a + 0.1 * fl * left[:, 3:4]
                b = b - 0.1 * fl * right[:, 3:4]
            out = out + jnp.where(lo, a, 0.0) + jnp.where(hi, b, 0.0)
            pred_ref[tile(i), :] = out
        first, second = pred_ref[tile(n), :], pred_ref[tile(NT + n), :]
        fp = jnp.where(row8 == 7, edge0[1, pl.ds(n, 1), :], pltpu.roll(first, 7, 0))
        fm = jnp.where(row8 == 0, edge0[0, pl.ds(n, 1), :], pltpu.roll(first, 1, 0))
        x = [v_ref[tile(NT + n), 0:128][:, 0:1],
             v_ref[tile(NT + n), cells - 128:cells][:, 127:128]]
        q = [p_ref[tile(n), 0:128][:, 0:1], p_ref[tile(n), cells - 128:cells][:, 127:128]]
        rows = pl.ds(n, 1)

        def corner(side, dn, up):
            return (jnp.where(row8 == 0, (side[:, 5:6] + 0.1 * side[:, 6:7]) * drecv[dn, rows, :][:, 1:2], 0.0)
                    + jnp.where(row8 == 7, side[:, 5:6] * drecv[up, rows, :][:, 1:2], 0.0))

        pl1 = (left[:, 4:5] + left[:, 5:6] * x[0] - 0.1 * left[:, 6:7] * q[0]
               + corner(left, 0, 2))
        pr1 = (right[:, 4:5] + right[:, 5:6] * x[1] + 0.1 * right[:, 6:7] * q[1]
               + corner(right, 1, 3))
        sp = jnp.where(hi, pr1, pltpu.roll(second, cells - 1, 1))
        sn = jnp.where(lo, pl1, pltpu.roll(second, 1, 1))
        sm = 0.1 * fl * (fp - fm + sp - sn)
        sm_ref[tile(n), :] = sm
        ap, am = a_pair(sm)
        rp, rm = r_pair(sm)
        rem = fl * (sm + (ap + am + rp + rm))
        gone = rem * mv
        kept = rem - gone
        at = pl.ds(pl.multiple_of(n * 16, 16), 16)
        for ref, x in ((stay, kept), (moved, gone)):
            top = x.astype(BF16).astype(F32)
            ref[at, :] = jnp.concatenate([top, x - top], 0).astype(BF16)
        e = jnp.where(lane128 == 0, sm[:, cells - 1:cells],
                      jnp.where(lane128 == 127, sm[:, 0:1] * left[:, 6:7], 0.0))
        e0 = jnp.sum(e[0:4], axis=0, keepdims=True)
        e1 = jnp.sum(e[4:8], axis=0, keepdims=True)
        bsend[tile(n), :] = jnp.where(row128 == 5, e0, jnp.where(row128 == 6, e1, 0.0))
        return 0

    lax.fori_loop(0, NT, complete, 0)

    def pieces(x):
        top = x.astype(BF16).astype(F32)
        return [top, x - top]

    zero7 = jnp.zeros((7, cells), F32)
    kept, gone = [], []
    for w, plane in ((0, 0), (1, 7)):
        x = jnp.concatenate([sm_ref[8 * i + plane:8 * i + plane + 1, :] for i in range(NT)], 0)
        x = x * trecv[w, 38:39, :]
        g = x * trecv[w, 37:38, :]
        for rows, y in ((kept, x - g), (gone, g)):
            for z in pieces(y):
                rows += [z, zero7]
    for ref, rows in ((stay, kept), (moved, gone)):
        for i in range(4):
            at = 16 * NT + 16 * i
            ref[at:at + 16, :] = jnp.concatenate(rows[2 * i:2 * i + 2], 0).astype(BF16)

    nt = (((1,), (1,)), ((), ()))
    tot = (lax.dot_general(stay[...], st1[0:128, :], nt, preferred_element_type=F32)
           + lax.dot_general(moved[...], st2[0:128, :], nt, preferred_element_type=F32))
    e_dn = tot[16 * NT:16 * NT + 16] + tot[16 * NT + 16:16 * NT + 32]
    e_up = tot[16 * NT + 32:16 * NT + 48] + tot[16 * NT + 48:16 * NT + 64]
    for n in range(NT):
        x = tot[16 * n:16 * n + 8] + tot[16 * n + 8:16 * n + 16]
        x0 = jnp.sum(x[0:4], axis=0, keepdims=True)
        x1 = jnp.sum(x[4:8], axis=0, keepdims=True)
        old = bsend[n * 8:n * 8 + 8, :]
        bsend[n * 8:n * 8 + 8, :] = jnp.where(
            row128 == 0, e_dn[n:n + 1], jnp.where(row128 == 1, x0, jnp.where(
                row128 == 2, x1, jnp.where(row128 == 3, e_up[n:n + 1], old))))
    bsend[72:74, :] = cd_ref[...]
    bsend[74:80, :] = jnp.zeros((6, 128), F32)
    for m, (dt, ds) in zip(mb, DIRS):
        there(ds, m.start)
    for m, (dt, ds) in zip(mb, DIRS):
        there(-ds, m.wait_recv)

    def keep(x, rows):
        return jnp.where((row128 >= rows[0]) & (row128 < rows[1]), x, 0.0)

    left_half = lane128 >= 64
    d0, d1 = jnp.zeros((8, 128), F32), jnp.zeros((8, 128), F32)
    for i, (dt, ds) in [(None, (0, 0))] + list(enumerate(DIRS)):
        x = bsend[72:80, :] if i is None else brecv[i, 72:80, :]
        ot, os = -dt, -ds
        x = keep(x, (1, 2) if ot == -2 else (0, 1) if ot == 2 else (0, 2))
        x = pltpu.roll(x, (3 + 2 * ot) % 8, 0)
        if os == 0:
            d0 = d0 + x
        else:
            d1 = d1 + jnp.where(left_half == (os < 0), x, 0.0)
    ok = jnp.where(left_half, (s > 0).astype(F32), (s < n_span - 1).astype(F32))
    inv = jnp.concatenate([0.8 / (4.0 + d0), ok * 0.8 / (4.0 + d1)], 1)

    def coarse(n, _):
        r0, r1 = jnp.zeros((8, 128), F32), jnp.zeros((8, 128), F32)
        for i, (dt, ds) in [(None, (0, 0))] + list(enumerate(DIRS)):
            x = bsend[tile(n), :] if i is None else brecv[i, tile(n), :]
            ot, os = -dt, -ds
            rows = (2, 4) if ot == -2 else (0, 2) if ot == 2 else (0, 4)
            sh = (2 * ot + 2) % 8
            main = pltpu.roll(keep(x, rows), sh, 0) if sh else keep(x, rows)
            side = pltpu.roll(keep(x, (rows[0] + 4, rows[1] + 4)), (sh + 4) % 8, 0) if (sh + 4) % 8 else keep(x, (rows[0] + 4, rows[1] + 4))
            if os == 0:
                r0, r1 = r0 + main, r1 + side
            else:
                r1 = r1 + jnp.where(left_half == (os < 0), main, 0.0)
                r0 = r0 + jnp.where(lane128 == (0 if os < 0 else 127), side, 0.0)
        rhs = jnp.concatenate([r0, r1], 1)
        x = inv * rhs
        for _ in range(CSWEEPS - 1):
            around = (pltpu.roll(x, 1, 0) + pltpu.roll(x, 7, 0)
                      + pltpu.roll(x, 1, 1) + pltpu.roll(x, 255, 1))
            x = 0.2 * x + inv * (rhs + around)
        mine = jnp.where(row128 < 4, x[3:4, 0:128], x[4:5, 0:128])
        top = mine.astype(BF16).astype(F32)
        lhs[tile(n), :] = jnp.concatenate([top, mine - top], 1)
        return 0

    lax.fori_loop(0, NT, coarse, 0)

    def lift(j, _):
        at = pl.ds(pl.multiple_of(j * width, width), width)
        x = lhs[...].astype(BF16)
        l1 = jnp.dot(x, st1[:, at], preferred_element_type=F32)
        l2 = jnp.dot(x, st2[:, at], preferred_element_type=F32)
        r = lax.broadcasted_iota(jnp.int32, (8, width), 1) + j * width
        f = (r < live * (cells // BLOCKS)).astype(F32)
        away = own_ref[:, at] != s * cols + r // FAN
        for n in range(NT):
            k = slice(n * 8, n * 8 + 8)
            corr_ref[k, at] = f * (sm_ref[k, at] + jnp.where(away, l2[k], l1[k]))
        return 0

    lax.fori_loop(0, cells // width, lift, 0)

    for m in m1 + m2:
        m.wait_send()
    for m, ds in list(zip(ms, (1, -1))) + [(m, d[1]) for m, d in zip(md, DIAG)] + [
            (m, d[1]) for m, d in zip(mb, DIRS)]:
        there(ds, m.wait_send)


def shards(n_theta, n_span, velocity, pressure, diffusivity, live_blocks, owner_map, coarse_diag):
    ncomp, ntime, planes, cells = velocity.shape
    vmem = pl.BlockSpec(memory_space=pltpu.VMEM)
    n = len(DIRS)
    pred, corr = pl.pallas_call(
        functools.partial(kernel, n_theta, n_span),
        out_shape=(
            jax.ShapeDtypeStruct((ncomp * ntime * planes, cells), F32),
            jax.ShapeDtypeStruct((ntime * planes, cells), F32),
        ),
        in_specs=[pl.BlockSpec(memory_space=pltpu.SMEM)] + [vmem] * 5,
        out_specs=(vmem, vmem),
        scratch_shapes=[
            pltpu.VMEM((2, 48, cells), F32),
            pltpu.VMEM((2, 48, cells), F32),
            pltpu.VMEM((2, 72, 128), F32),
            pltpu.VMEM((2, 72, 128), F32),
            pltpu.VMEM((4, 16, 128), F32),
            pltpu.VMEM((4, 16, 128), F32),
            pltpu.VMEM((80, 128), F32),
            pltpu.VMEM((n, 80, 128), F32),
            pltpu.VMEM((72, cells), F32),
            pltpu.VMEM((208, cells), BF16),
            pltpu.VMEM((208, cells), BF16),
            pltpu.VMEM((256, cells), BF16),
            pltpu.VMEM((256, cells), BF16),
            pltpu.VMEM((2, 9, cells), F32),
            pltpu.VMEM((72, 256), F32),
            pltpu.SemaphoreType.DMA((10 + n,)),
            pltpu.SemaphoreType.DMA((10 + n,)),
        ],
        compiler_params=pltpu.CompilerParams(
            collective_id=0, has_side_effects=True, vmem_limit_bytes=48 * 2**20),
    )(
        live_blocks,
        velocity.reshape(ncomp * ntime * planes, cells),
        pressure.reshape(ntime * planes, cells),
        diffusivity, owner_map, coarse_diag,
    )
    return pred.reshape(velocity.shape), corr.reshape(pressure.shape)


def solution(mesh):
    return jax.shard_map(
        functools.partial(shards, mesh.shape["theta"], mesh.shape["span"]),
        mesh=mesh,
        in_specs=(
            P(None, None, "theta", "span"),
            P(None, "theta", "span"),
            P("theta", "span"),
            P("theta", "span"),
            P("theta", "span"),
            P("theta", "span"),
        ),
        out_specs=(P(None, None, "theta", "span"), P(None, "theta", "span")),
        check_vma=False,
    )
```

time: 125 us -> 40 us (0.32)
  the two profiles are of different devices: /device:TPU:0 before, /device:TPU:17 now
where the time goes in v1:
time: 40 us; the launch traced here: 39.7 us
  Pallas kernels  31.4 us (78%)
  local copies, waits for them, and re-layouts  6.91 us (17%)
  between operations  1.3 us (3%)
    pallas_call x1, Pallas kernels, shards(): pl.pallas_call(functools.partial(kernel, n_theta, n_span), out_shape=(jax...  31.4 us
    unnamed x12, local copies, waits for them, and re-layouts  6.91 us

profile of v1, /device:TPU:17, one launch (start us, length us, event | category | flops | bytes accessed | tf_op | source)
XLA Modules:
  0.0 39.7 jit_solution(12405227249524940898)
XLA Ops:
  1.3 0.0 copy-start
  1.3 1.5 %copy-done = f32[3,9,8,2048]{3,2,1,0:T(8,128)S(1)} copy-done((f32[3,9,8,2048]{3,2,1,0:T(8,128)S(1)}, f32[3,9,8,2048]{3,2,1,0:T(8,128)}, u32[]{:S(2)}) %copy-start) | copy-done | bytes 1769496
  2.8 0.0 copy-start.1
  2.8 1.1 %copy-done.1 = f32[9,8,2048]{2,1,0:T(8,128)S(1)} copy-done((f32[9,8,2048]{2,1,0:T(8,128)S(1)}, f32[9,8,2048]{2,1,0:T(8,128)}, u32[]{:S(2)}) %copy-start.1) | copy-done | bytes 589848
  3.8 0.0 copy-start.2
  3.8 0.8 %copy-done.2 = f32[8,2048]{1,0:T(8,128)S(1)} copy-done((f32[8,2048]{1,0:T(8,128)S(1)}, f32[8,2048]{1,0:T(8,128)}, u32[]{:S(2)}) %copy-start.2) | copy-done | bytes 65560
  4.7 0.0 copy-start.3
  4.7 0.8 %copy-done.3 = s32[8,2048]{1,0:T(8,128)S(1)} copy-done((s32[8,2048]{1,0:T(8,128)S(1)}, s32[8,2048]{1,0:T(8,128)}, u32[]{:S(2)}) %copy-start.3) | copy-done | bytes 65560
  5.5 0.0 copy-start.4
  5.5 0.7 %copy-done.4 = f32[2,128]{1,0:T(2,128)S(1)} copy-done((f32[2,128]{1,0:T(2,128)S(1)}, f32[2,128]{1,0:T(2,128)}, u32[]{:S(2)}) %copy-start.4) | copy-done | bytes 1048
  6.2 31.4 %shard_map.77 = (f32[216,2048]{1,0:T(8,128)S(1)}, f32[72,2048]{1,0:T(8,128)S(1)}) custom-call(s32[1,1]{1,0:T(1,128)S(6)} %copy.10.live_ref, f32[216,2048]{1,0:T(8,128)S(1)} %bitcast.4, f32[72,2048]{1,0:T(8,128)S(1)} %bitcast.6, f32[8,2048]{1,0:T(8,128)S(1)} %copy-done.2, s32[8,2048]{1,0:T(8,128)S(1)} %copy-done.3, f32[2,128]{1,0:T(2,128)S(1)} %copy-done.4), custom_call_target="tpu_custom_call" | custom-call | tf_op jit(solution)/shard_map/pallas_call | solution.py:371
  37.6 1.2 %copy.11 = f32[3,9,8,2048]{3,2,1,0:T(8,128)} copy(f32[3,9,8,2048]{3,2,1,0:T(8,128)S(1)} %bitcast.5) | data formatting | bytes 3538944
  38.8 0.8 %copy.12 = f32[9,8,2048]{2,1,0:T(8,128)} copy(f32[9,8,2048]{2,1,0:T(8,128)S(1)} %bitcast.7) | data formatting | bytes 1179648
Async XLA Ops:
  1.3 1.5 %copy-start = (f32[3,9,8,2048]{3,2,1,0:T(8,128)S(1)}, f32[3,9,8,2048]{3,2,1,0:T(8,128)}, u32[]{:S(2)}) copy-start(f32[3,9,8,2048]{3,2,1,0:T(8,128)} %param.6) | copy-start | bytes 5308420
  2.8 1.1 %copy-start.1 = (f32[9,8,2048]{2,1,0:T(8,128)S(1)}, f32[9,8,2048]{2,1,0:T(8,128)}, u32[]{:S(2)}) copy-start(f32[9,8,2048]{2,1,0:T(8,128)} %param.7) | copy-start | bytes 1769476
  3.8 0.8 %copy-start.2 = (f32[8,2048]{1,0:T(8,128)S(1)}, f32[8,2048]{1,0:T(8,128)}, u32[]{:S(2)}) copy-start(f32[8,2048]{1,0:T(8,128)} %d_ref.1) | copy-start | bytes 196612
  4.7 0.8 %copy-start.3 = (s32[8,2048]{1,0:T(8,128)S(1)}, s32[8,2048]{1,0:T(8,128)}, u32[]{:S(2)}) copy-start(s32[8,2048]{1,0:T(8,128)} %own_ref.1) | copy-start | bytes 196612
  5.5 0.7 %copy-start.4 = (f32[2,128]{1,0:T(2,128)S(1)}, f32[2,128]{1,0:T(2,128)}, u32[]{:S(2)}) copy-start(f32[2,128]{1,0:T(2,128)} %cd_ref.1) | copy-start | bytes 3076

commit v2 on v1

--- a/solution.py
+++ b/solution.py
@@ -26,15 +26,23 @@
 
 def kernel(
     n_theta, n_span,
-    live_ref, v_ref, p_ref, d_ref, own_ref, cd_ref,
-    pred_ref, corr_ref,
+    live_ref, v_hbm, p_hbm, d_hbm, own_hbm, cd_hbm,
+    pred_ref, sm_ref, lhs,
+    v_ref, p_ref, d_ref, own_ref, cd_ref,
     tsend, trecv, ssend, srecv, dsend, drecv, bsend, brecv,
-    sm_ref, stay, moved, st1, st2, edge0, lhs,
-    send_sem, recv_sem,
+    psend, precv, side_ref, stay, moved, st1, st2, edge0,
+    send_sem, recv_sem, load_sem,
 ):
     cells = v_ref.shape[1]
     cols = cells // FAN
     t, s = lax.axis_index("theta"), lax.axis_index("span")
+    third = NT * 8
+    loads = [pltpu.make_async_copy(v_hbm.at[third * c:third * c + third], v_ref.at[third * c:third * c + third],
+                                   load_sem.at[c]) for c in range(3)]
+    loads += [pltpu.make_async_copy(a, b, load_sem.at[3 + i]) for i, (a, b) in enumerate((
+        (p_hbm, p_ref), (d_hbm, d_ref), (own_hbm, own_ref), (cd_hbm, cd_ref)))]
+    for m in loads:
+        m.start()
     tile = lambda i: pl.ds(pl.multiple_of(i * 8, 8), 8)
 
     def peer(dt, ds):
@@ -62,9 +70,10 @@
     row8 = lax.broadcasted_iota(jnp.int32, (8, 1), 0)
     lane128 = lax.broadcasted_iota(jnp.int32, (8, 128), 1)
     row128 = lax.broadcasted_iota(jnp.int32, (8, 128), 0)
-    live = live_ref[0, 0]
-    fl = (lane < live * (cells // BLOCKS)).astype(F32)
-    base = s * cols + lane // FAN
+    for m in loads:
+        m.wait()
+    fl = (lane < live_ref[0, 0] * (cells // BLOCKS)).astype(F32)
+    base = s * cols + (lane >> 4)
     mv = (own_ref[...] != base).astype(F32)
     df = d_ref[...] * (0.1 * fl)
 
@@ -93,7 +102,9 @@
     m2 = [remote(tsend.at[w, 32:48], trecv.at[w, 32:48], 2 + w, 1 - 2 * w, 0) for w in range(2)]
     ms = [remote(ssend.at[w], srecv.at[w], 4 + w, 0, 1 - 2 * w) for w in range(2)]
     md = [remote(dsend.at[i], drecv.at[i], 6 + i, dt, ds) for i, (dt, ds) in enumerate(DIAG)]
-    mb = [remote(bsend, brecv.at[i], 10 + i, dt, ds) for i, (dt, ds) in enumerate(DIRS)]
+    mb = [remote(bsend, brecv.at[i], 10 + i, dt, ds) if ds == 0 else
+          remote(psend.at[(1 - ds) // 2], precv.at[i - 4], 10 + i, dt, ds)
+          for i, (dt, ds) in enumerate(DIRS)]
     for m in m1:
         m.start()
     for m, (dt, ds) in zip(md, DIAG):
@@ -107,7 +118,7 @@
                 drecv[i] = jnp.zeros(drecv.shape[1:], F32)
         for i, (_, e) in enumerate(DIRS):
             if e == -ds:
-                brecv[i] = jnp.zeros(brecv.shape[1:], F32)
+                precv[i - 4] = jnp.zeros(precv.shape[1:], F32)
 
     pl.when(s == 0)(lambda: clear(-1))
     pl.when(s == n_span - 1)(lambda: clear(1))
@@ -174,10 +185,10 @@
 
     def members(j, _):
         at = pl.ds(pl.multiple_of(j * width, width), width)
-        r = lax.broadcasted_iota(jnp.int32, (256, width), 1) + j * width
-        k = lax.broadcasted_iota(jnp.int32, (256, width), 0) & 127
-        b = r // FAN
-        e = r % FAN
+        r = lax.broadcasted_iota(jnp.int32, (128, width), 1) + j * width
+        k = lax.broadcasted_iota(jnp.int32, (128, width), 0)
+        b = r >> 4
+        e = r & (FAN - 1)
         to = jnp.where(e == 0, b - 1, jnp.where(e == FAN - 1, b + 1, -9))
         st1[:, at] = (b == k).astype(F32).astype(BF16)
         st2[:, at] = (to == k).astype(F32).astype(BF16)
@@ -213,15 +224,16 @@
             i = c * NT + n
             out = (pred_ref[tile(i), :] + w_dn * trecv[0, pl.ds(i, 1), :]
                    + w_up * trecv[1, pl.ds(i, 1), :])
-            a, b = df * left[:, c:c + 1], df * right[:, c:c + 1]
             if c == 0:
                 out = (out + q_dn * trecv[0, pl.ds(27 + n, 1), :]
                        - q_up * trecv[1, pl.ds(27 + n, 1), :])
-            if c == 1:
-                a = a + 0.1 * fl * left[:, 3:4]
-                b = b - 0.1 * fl * right[:, 3:4]
-            out = out + jnp.where(lo, a, 0.0) + jnp.where(hi, b, 0.0)
             pred_ref[tile(i), :] = out
+            for c0, col, side, sign in ((0, 0, left, 0.1), (cells - 128, 127, right, -0.1)):
+                at = slice(c0, c0 + 128)
+                x = df[:, at] * side[:, c:c + 1]
+                if c == 1:
+                    x = x + sign * fl[:, at] * side[:, 3:4]
+                pred_ref[tile(i), at] += jnp.where(lane128 == col, x, 0.0)
         first, second = pred_ref[tile(n), :], pred_ref[tile(NT + n), :]
         fp = jnp.where(row8 == 7, edge0[1, pl.ds(n, 1), :], pltpu.roll(first, 7, 0))
         fm = jnp.where(row8 == 0, edge0[0, pl.ds(n, 1), :], pltpu.roll(first, 1, 0))
@@ -255,7 +267,7 @@
                       jnp.where(lane128 == 127, sm[:, 0:1] * left[:, 6:7], 0.0))
         e0 = jnp.sum(e[0:4], axis=0, keepdims=True)
         e1 = jnp.sum(e[4:8], axis=0, keepdims=True)
-        bsend[tile(n), :] = jnp.where(row128 == 5, e0, jnp.where(row128 == 6, e1, 0.0))
+        side_ref[tile(n), :] = jnp.where(row128 == 5, e0, jnp.where(row128 == 6, e1, 0.0))
         return 0
 
     lax.fori_loop(0, NT, complete, 0)
@@ -279,20 +291,31 @@
             ref[at:at + 16, :] = jnp.concatenate(rows[2 * i:2 * i + 2], 0).astype(BF16)
 
     nt = (((1,), (1,)), ((), ()))
-    tot = (lax.dot_general(stay[...], st1[0:128, :], nt, preferred_element_type=F32)
-           + lax.dot_general(moved[...], st2[0:128, :], nt, preferred_element_type=F32))
+    tot = (lax.dot_general(stay[...], st1[...], nt, preferred_element_type=F32)
+           + lax.dot_general(moved[...], st2[...], nt, preferred_element_type=F32))
     e_dn = tot[16 * NT:16 * NT + 16] + tot[16 * NT + 16:16 * NT + 32]
     e_up = tot[16 * NT + 32:16 * NT + 48] + tot[16 * NT + 48:16 * NT + 64]
+    pack_r, pack_l = jnp.zeros((8, 128), F32), jnp.zeros((8, 128), F32)
+    main, sides = [], jnp.zeros((8, 128), F32)
     for n in range(NT):
         x = tot[16 * n:16 * n + 8] + tot[16 * n + 8:16 * n + 16]
         x0 = jnp.sum(x[0:4], axis=0, keepdims=True)
         x1 = jnp.sum(x[4:8], axis=0, keepdims=True)
-        old = bsend[n * 8:n * 8 + 8, :]
-        bsend[n * 8:n * 8 + 8, :] = jnp.where(
-            row128 == 0, e_dn[n:n + 1], jnp.where(row128 == 1, x0, jnp.where(
-                row128 == 2, x1, jnp.where(row128 == 3, e_up[n:n + 1], old))))
-    bsend[72:74, :] = cd_ref[...]
-    bsend[74:80, :] = jnp.zeros((6, 128), F32)
+        x = jnp.where(row128 == 0, e_dn[n:n + 1], jnp.where(row128 == 1, x0, jnp.where(
+            row128 == 2, x1, jnp.where(row128 == 3, e_up[n:n + 1], side_ref[n * 8:n * 8 + 8, :]))))
+        main.append(x)
+        slot = (lane128 >> 2) == n
+        pack_r = jnp.where(slot, pltpu.roll(x, 3 + 4 * n, 1), pack_r)
+        pack_l = jnp.where(slot, pltpu.roll(x, 1 + 4 * n, 1), pack_l)
+        sides = jnp.where((lane128 >> 1) == n, pltpu.roll(x, 1 + 2 * n, 1), sides)
+    cd = jnp.concatenate([cd_ref[...], jnp.zeros((6, 128), F32)], 0)
+    for i in range(5):
+        y = main[2 * i + 1] if 2 * i + 1 < NT else jnp.zeros((8, 128), F32)
+        bsend[8 * i:8 * i + 8, :] = jnp.where(row128 < 4, main[2 * i], pltpu.roll(y, 4, 0))
+    bsend[40:48, :] = jnp.where(row128 < 4, cd, sides)
+    cslot = (lane128 >> 2) == 10
+    psend[0] = jnp.where(cslot, pltpu.roll(cd, 43, 1), pack_r)
+    psend[1] = jnp.where(cslot, pltpu.roll(cd, 41, 1), pack_l)
     for m, (dt, ds) in zip(mb, DIRS):
         there(ds, m.start)
     for m, (dt, ds) in zip(mb, DIRS):
@@ -301,34 +324,40 @@
     def keep(x, rows):
         return jnp.where((row128 >= rows[0]) & (row128 < rows[1]), x, 0.0)
 
-    left_half = lane128 >= 64
-    d0, d1 = jnp.zeros((8, 128), F32), jnp.zeros((8, 128), F32)
-    for i, (dt, ds) in [(None, (0, 0))] + list(enumerate(DIRS)):
-        x = bsend[72:80, :] if i is None else brecv[i, 72:80, :]
-        ot, os = -dt, -ds
-        x = keep(x, (1, 2) if ot == -2 else (0, 1) if ot == 2 else (0, 2))
-        x = pltpu.roll(x, (3 + 2 * ot) % 8, 0)
-        if os == 0:
-            d0 = d0 + x
-        else:
-            d1 = d1 + jnp.where(left_half == (os < 0), x, 0.0)
-    ok = jnp.where(left_half, (s > 0).astype(F32), (s < n_span - 1).astype(F32))
+    def turn(x, by, axis):
+        return pltpu.roll(x, by % x.shape[axis], axis) if by % x.shape[axis] else x
+
+    def rows_of(ot):
+        return (2, 4) if ot == -2 else (0, 2) if ot == 2 else (0, 4)
+
+    def diag_rows(x, ot):
+        return turn(keep(x, (1, 2) if ot == -2 else (0, 1) if ot == 2 else (0, 2)), 3 + 2 * ot, 0)
+
+    near = [(0, bsend)] + [(-dt, brecv.at[i]) for i, (dt, ds) in enumerate(DIRS) if ds == 0]
+    d0 = sum(diag_rows(ref[40:48, :], ot) for ot, ref in near)
+    beside = []
+    for sent in (1, -1):
+        got = [(-dt, precv[i - 4]) for i, (dt, ds) in enumerate(DIRS) if ds == sent]
+        beside.append((
+            sum(turn(keep(x, rows_of(ot)), 2 * ot + 2, 0) for ot, x in got),
+            sum(turn(keep(x, (rows_of(ot)[0] + 4, rows_of(ot)[1] + 4)), 2 * ot + 6, 0) for ot, x in got),
+            sum(diag_rows(x, ot) for ot, x in got)))
+    s_near = sum(turn(keep(ref[40:48, :], (rows_of(ot)[0] + 4, rows_of(ot)[1] + 4)), 2 * ot + 6, 0)
+                 for ot, ref in near)
+    (ml, sl, dl), (mr, sr, dr) = beside
+    from_left, from_right = lane128 >= 125, lane128 <= 2
+    d1 = (jnp.where(from_left, turn(dl, -43, 1), 0.0) + jnp.where(from_right, turn(dr, -41, 1), 0.0))
+    ok = jnp.where(lane128 >= 64, (s > 0).astype(F32), (s < n_span - 1).astype(F32))
     inv = jnp.concatenate([0.8 / (4.0 + d0), ok * 0.8 / (4.0 + d1)], 1)
-
-    def coarse(n, _):
-        r0, r1 = jnp.zeros((8, 128), F32), jnp.zeros((8, 128), F32)
-        for i, (dt, ds) in [(None, (0, 0))] + list(enumerate(DIRS)):
-            x = bsend[tile(n), :] if i is None else brecv[i, tile(n), :]
-            ot, os = -dt, -ds
-            rows = (2, 4) if ot == -2 else (0, 2) if ot == 2 else (0, 4)
-            sh = (2 * ot + 2) % 8
-            main = pltpu.roll(keep(x, rows), sh, 0) if sh else keep(x, rows)
-            side = pltpu.roll(keep(x, (rows[0] + 4, rows[1] + 4)), (sh + 4) % 8, 0) if (sh + 4) % 8 else keep(x, (rows[0] + 4, rows[1] + 4))
-            if os == 0:
-                r0, r1 = r0 + main, r1 + side
-            else:
-                r1 = r1 + jnp.where(left_half == (os < 0), main, 0.0)
-                r0 = r0 + jnp.where(lane128 == (0 if os < 0 else 127), side, 0.0)
+    for n in range(NT):
+        lo4 = 4 * (n % 2)
+        r0 = sum(turn(keep(ref[8 * (n // 2):8 * (n // 2) + 8, :], (rows_of(ot)[0] + lo4, rows_of(ot)[1] + lo4)),
+                      2 * ot + 2 - lo4, 0) for ot, ref in near)
+        r0 = r0 + jnp.where(lane128 == 0, turn(sl, -(3 + 4 * n), 1), 0.0)
+        r0 = r0 + jnp.where(lane128 == 127, turn(sr, -(1 + 4 * n), 1), 0.0)
+        r1 = jnp.where((lane128 == 0) | (lane128 == 127), turn(s_near, -(1 + 2 * n), 1), 0.0)
+        r1 = r1 + jnp.where(from_left, turn(ml, -(3 + 4 * n), 1), 0.0)
+        r1 = r1 + jnp.where(from_right, turn(mr, -(1 + 4 * n), 1), 0.0)
         rhs = jnp.concatenate([r0, r1], 1)
         x = inv * rhs
         for _ in range(CSWEEPS - 1):
@@ -337,25 +366,7 @@
             x = 0.2 * x + inv * (rhs + around)
         mine = jnp.where(row128 < 4, x[3:4, 0:128], x[4:5, 0:128])
         top = mine.astype(BF16).astype(F32)
-        lhs[tile(n), :] = jnp.concatenate([top, mine - top], 1)
-        return 0
-
-    lax.fori_loop(0, NT, coarse, 0)
-
-    def lift(j, _):
-        at = pl.ds(pl.multiple_of(j * width, width), width)
-        x = lhs[...].astype(BF16)
-        l1 = jnp.dot(x, st1[:, at], preferred_element_type=F32)
-        l2 = jnp.dot(x, st2[:, at], preferred_element_type=F32)
-        r = lax.broadcasted_iota(jnp.int32, (8, width), 1) + j * width
-        f = (r < live * (cells // BLOCKS)).astype(F32)
-        away = own_ref[:, at] != s * cols + r // FAN
-        for n in range(NT):
-            k = slice(n * 8, n * 8 + 8)
-            corr_ref[k, at] = f * (sm_ref[k, at] + jnp.where(away, l2[k], l1[k]))
-        return 0
-
-    lax.fori_loop(0, cells // width, lift, 0)
+        lhs[n * 8:n * 8 + 8, :] = jnp.concatenate([top, mine - top], 1)
 
     for m in m1 + m2:
         m.wait_send()
@@ -364,45 +375,109 @@
         there(ds, m.wait_send)
 
 
+def lift_kernel(live_ref, raw_ref, sm_ref, lhs, own_hbm, pred_hbm, corr_hbm, own_ref, corr, sems):
+    cells = own_ref.shape[1]
+    width = 256
+    count = cells // width
+    pred_out = pltpu.make_async_copy(raw_ref, pred_hbm, sems.at[0])
+    pred_out.start()
+    own_in = pltpu.make_async_copy(own_hbm, own_ref, sems.at[1])
+    own_in.start()
+    first = lax.axis_index("span") * (cells // FAN)
+    x = lhs[...].astype(BF16)
+    own_in.wait()
+    live = live_ref[0, 0]
+    outs = []
+    for j in range(count):
+        at = slice(j * width, j * width + width)
+        r = lax.broadcasted_iota(jnp.int32, (256, width), 1) + j * width
+        k = lax.broadcasted_iota(jnp.int32, (256, width), 0) & 127
+        b = r >> 4
+        e = r & (FAN - 1)
+        to = jnp.where(e == 0, b - 1, jnp.where(e == FAN - 1, b + 1, -9))
+        l1 = jnp.dot(x, (b == k).astype(F32).astype(BF16), preferred_element_type=F32)
+        l2 = jnp.dot(x, (to == k).astype(F32).astype(BF16), preferred_element_type=F32)
+        r = lax.broadcasted_iota(jnp.int32, (8, width), 1) + j * width
+        f = (r < live * (cells // BLOCKS)).astype(F32)
+        away = own_ref[:, at] != first + (r >> 4)
+        for n in range(NT):
+            k = slice(n * 8, n * 8 + 8)
+            corr[k, at] = f * (sm_ref[k, at] + jnp.where(away, l2[k], l1[k]))
+        if j % 2:
+            at = slice(j * width - width, j * width + width)
+            outs.append(pltpu.make_async_copy(corr.at[:, at], corr_hbm.at[:, at], sems.at[2 + j // 2]))
+            outs[-1].start()
+    for m in outs + [pred_out]:
+        m.wait()
+
+
 def shards(n_theta, n_span, velocity, pressure, diffusivity, live_blocks, owner_map, coarse_diag):
     ncomp, ntime, planes, cells = velocity.shape
     vmem = pl.BlockSpec(memory_space=pltpu.VMEM)
+    hbm = pl.BlockSpec(memory_space=pltpu.HBM)
+    smem = pl.BlockSpec(memory_space=pltpu.SMEM)
     n = len(DIRS)
-    pred, corr = pl.pallas_call(
+    rows = ntime * planes
+    pin = lambda x: pltpu.with_memory_space_constraint(x, pltpu.HBM)
+    own, live = pin(owner_map), live_blocks
+    raw, sm, lhs = pl.pallas_call(
         functools.partial(kernel, n_theta, n_span),
         out_shape=(
-            jax.ShapeDtypeStruct((ncomp * ntime * planes, cells), F32),
-            jax.ShapeDtypeStruct((ntime * planes, cells), F32),
+            jax.ShapeDtypeStruct((ncomp * rows, cells), F32),
+            jax.ShapeDtypeStruct((rows, cells), F32),
+            jax.ShapeDtypeStruct((rows, 256), F32),
         ),
-        in_specs=[pl.BlockSpec(memory_space=pltpu.SMEM)] + [vmem] * 5,
-        out_specs=(vmem, vmem),
+        in_specs=[smem] + [hbm] * 5,
+        out_specs=(vmem, vmem, vmem),
         scratch_shapes=[
+            pltpu.VMEM((ncomp * rows, cells), F32),
+            pltpu.VMEM((rows, cells), F32),
+            pltpu.VMEM((planes, cells), F32),
+            pltpu.VMEM((planes, cells), jnp.int32),
+            pltpu.VMEM(coarse_diag.shape, F32),
             pltpu.VMEM((2, 48, cells), F32),
             pltpu.VMEM((2, 48, cells), F32),
             pltpu.VMEM((2, 72, 128), F32),
             pltpu.VMEM((2, 72, 128), F32),
             pltpu.VMEM((4, 16, 128), F32),
             pltpu.VMEM((4, 16, 128), F32),
-            pltpu.VMEM((80, 128), F32),
-            pltpu.VMEM((n, 80, 128), F32),
-            pltpu.VMEM((72, cells), F32),
+            pltpu.VMEM((48, 128), F32),
+            pltpu.VMEM((4, 48, 128), F32),
+            pltpu.VMEM((2, 8, 128), F32),
+            pltpu.VMEM((10, 8, 128), F32),
+            pltpu.VMEM((72, 128), F32),
             pltpu.VMEM((208, cells), BF16),
             pltpu.VMEM((208, cells), BF16),
-            pltpu.VMEM((256, cells), BF16),
-            pltpu.VMEM((256, cells), BF16),
+            pltpu.VMEM((128, cells), BF16),
+            pltpu.VMEM((128, cells), BF16),
             pltpu.VMEM((2, 9, cells), F32),
-            pltpu.VMEM((72, 256), F32),
             pltpu.SemaphoreType.DMA((10 + n,)),
             pltpu.SemaphoreType.DMA((10 + n,)),
+            pltpu.SemaphoreType.DMA((7,)),
         ],
         compiler_params=pltpu.CompilerParams(
-            collective_id=0, has_side_effects=True, vmem_limit_bytes=48 * 2**20),
+            collective_id=0, has_side_effects=True, vmem_limit_bytes=40 * 2**20),
     )(
-        live_blocks,
-        velocity.reshape(ncomp * ntime * planes, cells),
-        pressure.reshape(ntime * planes, cells),
-        diffusivity, owner_map, coarse_diag,
+        live,
+        pin(velocity.reshape(ncomp * rows, cells)),
+        pin(pressure.reshape(rows, cells)),
+        pin(diffusivity), own, pin(coarse_diag),
     )
+    pred, corr = pl.pallas_call(
+        lift_kernel,
+        out_shape=(
+            jax.ShapeDtypeStruct((ncomp * rows, cells), F32),
+            jax.ShapeDtypeStruct((rows, cells), F32),
+        ),
+        in_specs=[smem, vmem, vmem, vmem, hbm],
+        out_specs=(hbm, hbm),
+        scratch_shapes=[
+            pltpu.VMEM((planes, cells), jnp.int32),
+            pltpu.VMEM((rows, cells), F32),
+            pltpu.SemaphoreType.DMA((8,)),
+        ],
+        compiler_params=pltpu.CompilerParams(vmem_limit_bytes=24 * 2**20),
+    )(live, raw, sm, lhs, own)
     return pred.reshape(velocity.shape), corr.reshape(pressure.shape)
 
 

time: 40 us -> 27.6 us (0.69)
  the two profiles are of different devices: /device:TPU:17 before, /device:TPU:0 now
where the time goes in v2:
time: 27.6 us; the launch traced here: 27.4 us
  Pallas kernels  26.1 us (95%)
  between operations  1.29 us (5%)
    pallas_call x1, Pallas kernels, shards(): pl.pallas_call(functools.partial(kernel, n_theta, n_span), out_shape=(jax...  24 us
    pallas_call x1, Pallas kernels, shards(): pl.pallas_call(lift_kernel, out_shape=(jax.ShapeDtypeStruct((ncomp * rows...  2.12 us

profile of v2, /device:TPU:0, one launch (start us, length us, event | category | flops | bytes accessed | tf_op | source)
XLA Modules:
  0.0 27.4 jit_solution(4052924794623099037)
XLA Ops:
  1.3 24.0 %shard_map.77 = (f32[216,2048]{1,0:T(8,128)S(1)}, f32[72,2048]{1,0:T(8,128)S(1)}, f32[72,256]{1,0:T(8,128)S(1)}) custom-call(s32[1,1]{1,0:T(1,128)S(6)} %copy.8.live_ref, f32[216,2048]{1,0:T(8,128)} %bitcast.4, f32[72,2048]{1,0:T(8,128)} %bitcast.5, f32[8,2048]{1,0:T(8,128)} %d_hbm.1, s32[8,2048]{1,0:T(8,128)} %own_hbm.3, f32[2,128]{1,0:T(2,128)} %cd_hbm.1), custom_call_target="tpu_custom_call" | custom-call | tf_op jit(solution)/shard_map/pallas_call | solution.py:423
  25.3 2.1 %shard_map.78 = (f32[216,2048]{1,0:T(8,128)}, f32[72,2048]{1,0:T(8,128)}) custom-call(s32[1,1]{1,0:T(1,128)S(6)} %copy.8.live_ref, f32[216,2048]{1,0:T(8,128)S(1)} %get-tuple-element.7.raw_ref, f32[72,2048]{1,0:T(8,128)S(1)} %get-tuple-element.8.sm_ref, f32[72,256]{1,0:T(8,128)S(1)} %get-tuple-element.9.lhs, s32[8,2048]{1,0:T(8,128)} %own_hbm.3), custom_call_target="tpu_custom_call" | custom-call | tf_op jit(solution)/shard_map/pallas_call | solution.py:466

commit v3 on v2

--- a/solution.py
+++ b/solution.py
@@ -20,6 +20,7 @@
 DIRS = [(1, 0), (-1, 0), (2, 0), (-2, 0)] + [
     (dt, ds) for ds in (1, -1) for dt in (0, 1, -1, 2, -2)
 ]
+NEAR = [(dt, ds) for dt in (0, 1, -1) for ds in (0, 1, -1) if dt or ds]
 DIAG = [(1, 1), (1, -1), (-1, 1), (-1, -1)]
 FREQ = [0.15 * (-1.0) ** d / math.sin(math.pi * d / NT) for d in range(1, 5)]
 
@@ -62,7 +63,7 @@
             device_id=peer(dt, ds), device_id_type=MESH)
 
     barrier = pltpu.get_barrier_semaphore()
-    for dt, ds in DIRS:
+    for dt, ds in NEAR:
         there(ds, lambda dt=dt, ds=ds: pl.semaphore_signal(
             barrier, inc=1, device_id=peer(dt, ds), device_id_type=MESH))
 
@@ -96,7 +97,7 @@
         l9 = lax.broadcasted_iota(jnp.int32, (9, 128), 1)
         dsend[i, 0:9, :] = jnp.where(l9 == 0, a0, a1)
 
-    pl.semaphore_wait(barrier, jnp.where((s > 0) & (s < n_span - 1), 14, 9))
+    pl.semaphore_wait(barrier, jnp.where((s > 0) & (s < n_span - 1), 8, 5))
 
     m1 = [remote(tsend.at[w, 0:32], trecv.at[w, 0:32], w, 1 - 2 * w, 0) for w in range(2)]
     m2 = [remote(tsend.at[w, 32:48], trecv.at[w, 32:48], 2 + w, 1 - 2 * w, 0) for w in range(2)]
@@ -218,23 +219,28 @@
     q_dn = jnp.where(row8 == 0, 0.1 * fl, 0.0)
     q_up = jnp.where(row8 == 7, 0.1 * fl, 0.0)
 
+    def completed(n, c, left, right):
+        i = c * NT + n
+        out = (pred_ref[tile(i), :] + w_dn * trecv[0, pl.ds(i, 1), :]
+               + w_up * trecv[1, pl.ds(i, 1), :])
+        if c == 0:
+            out = (out + q_dn * trecv[0, pl.ds(27 + n, 1), :]
+                   - q_up * trecv[1, pl.ds(27 + n, 1), :])
+        ends = []
+        for c0, col, side, sign in ((0, 0, left, 0.1), (cells - 128, 127, right, -0.1)):
+            at = slice(c0, c0 + 128)
+            x = df[:, at] * side[:, c:c + 1]
+            if c == 1:
+                x = x + sign * fl[:, at] * side[:, 3:4]
+            ends.append(out[:, at] + jnp.where(lane128 == col, x, 0.0))
+        out = jnp.concatenate([ends[0], out[:, 128:cells - 128], ends[1]], 1)
+        pred_ref[tile(i), :] = out
+        return out
+
     def complete(n, _):
         left, right = srecv[0, tile(n), :], srecv[1, tile(n), :]
-        for c in range(3):
-            i = c * NT + n
-            out = (pred_ref[tile(i), :] + w_dn * trecv[0, pl.ds(i, 1), :]
-                   + w_up * trecv[1, pl.ds(i, 1), :])
-            if c == 0:
-                out = (out + q_dn * trecv[0, pl.ds(27 + n, 1), :]
-                       - q_up * trecv[1, pl.ds(27 + n, 1), :])
-            pred_ref[tile(i), :] = out
-            for c0, col, side, sign in ((0, 0, left, 0.1), (cells - 128, 127, right, -0.1)):
-                at = slice(c0, c0 + 128)
-                x = df[:, at] * side[:, c:c + 1]
-                if c == 1:
-                    x = x + sign * fl[:, at] * side[:, 3:4]
-                pred_ref[tile(i), at] += jnp.where(lane128 == col, x, 0.0)
-        first, second = pred_ref[tile(n), :], pred_ref[tile(NT + n), :]
+        first = completed(n, 0, left, right)
+        second = completed(n, 1, left, right)
         fp = jnp.where(row8 == 7, edge0[1, pl.ds(n, 1), :], pltpu.roll(first, 7, 0))
         fm = jnp.where(row8 == 0, edge0[0, pl.ds(n, 1), :], pltpu.roll(first, 1, 0))
         x = [v_ref[tile(NT + n), 0:128][:, 0:1],
@@ -270,7 +276,7 @@
         side_ref[tile(n), :] = jnp.where(row128 == 5, e0, jnp.where(row128 == 6, e1, 0.0))
         return 0
 
-    lax.fori_loop(0, NT, complete, 0)
+    lax.fori_loop(0, NT, complete, 0, unroll=3)
 
     def pieces(x):
         top = x.astype(BF16).astype(F32)
@@ -316,8 +322,14 @@
     cslot = (lane128 >> 2) == 10
     psend[0] = jnp.where(cslot, pltpu.roll(cd, 43, 1), pack_r)
     psend[1] = jnp.where(cslot, pltpu.roll(cd, 41, 1), pack_l)
-    for m, (dt, ds) in zip(mb, DIRS):
+    for m, (dt, ds) in sorted(zip(mb, DIRS), key=lambda x: -abs(x[1][0]) - abs(x[1][1])):
         there(ds, m.start)
+
+    def third_component(n, _):
+        completed(n, 2, srecv[0, tile(n), :], srecv[1, tile(n), :])
+        return 0
+
+    lax.fori_loop(0, NT, third_component, 0)
     for m, (dt, ds) in zip(mb, DIRS):
         there(-ds, m.wait_recv)
 

time: 27.6 us -> 26.8 us (0.971)
  Pallas kernels: 26.1 us -> 25.3 us
    pallas_call x1, Pallas kernels: 24 us -> 23.2 us  [shards(): pl.pallas_call(functools.partial(kernel, n_theta, n_span), out_shape=(jax...]
where the time goes in v3:
time: 26.8 us; the launch traced here: 26.6 us
  Pallas kernels  25.3 us (94%)
  between operations  1.29 us (5%)
    pallas_call x1, Pallas kernels, shards(): pl.pallas_call(functools.partial(kernel, n_theta, n_span), out_shape=(jax...  23.2 us
    pallas_call x1, Pallas kernels, shards(): pl.pallas_call(lift_kernel, out_shape=(jax.ShapeDtypeStruct((ncomp * rows...  2.12 us

profile of v3, /device:TPU:0, one launch (start us, length us, event | category | flops | bytes accessed | tf_op | source)
XLA Modules:
  0.0 26.6 jit_solution(10546148623701331778)
XLA Ops:
  1.3 23.2 %shard_map.77 = (f32[216,2048]{1,0:T(8,128)S(1)}, f32[72,2048]{1,0:T(8,128)S(1)}, f32[72,256]{1,0:T(8,128)S(1)}) custom-call(s32[1,1]{1,0:T(1,128)S(6)} %copy.8.live_ref, f32[216,2048]{1,0:T(8,128)} %bitcast.4, f32[72,2048]{1,0:T(8,128)} %bitcast.5, f32[8,2048]{1,0:T(8,128)} %d_hbm.1, s32[8,2048]{1,0:T(8,128)} %own_hbm.3, f32[2,128]{1,0:T(2,128)} %cd_hbm.1), custom_call_target="tpu_custom_call" | custom-call | tf_op jit(solution)/shard_map/pallas_call | solution.py:435
  24.5 2.1 %shard_map.78 = (f32[216,2048]{1,0:T(8,128)}, f32[72,2048]{1,0:T(8,128)}) custom-call(s32[1,1]{1,0:T(1,128)S(6)} %copy.8.live_ref, f32[216,2048]{1,0:T(8,128)S(1)} %get-tuple-element.7.raw_ref, f32[72,2048]{1,0:T(8,128)S(1)} %get-tuple-element.8.sm_ref, f32[72,256]{1,0:T(8,128)S(1)} %get-tuple-element.9.lhs, s32[8,2048]{1,0:T(8,128)} %own_hbm.3), custom_call_target="tpu_custom_call" | custom-call | tf_op jit(solution)/shard_map/pallas_call | solution.py:478

commit v4 on v3

--- a/solution.py
+++ b/solution.py
@@ -78,16 +78,18 @@
     mv = (own_ref[...] != base).astype(F32)
     df = d_ref[...] * (0.1 * fl)
 
-    def pack(way, row, ref, plane, count):
+    def pack(way, row, ref, plane, count, first=0):
         for i in range(count):
-            tsend[way, row + i:row + i + 1, :] = ref[8 * i + plane:8 * i + plane + 1, :]
+            at = 8 * (first + i) + plane
+            tsend[way, row + i:row + i + 1, :] = ref[at:at + 1, :]
 
     for way, plane in ((0, 7), (1, 0)):
-        pack(way, 0, v_ref, plane, 27)
-        pack(way, 27, p_ref, plane, 9)
-        tsend[way, 36:37, :] = df[plane:plane + 1, :]
-        tsend[way, 37:38, :] = mv[plane:plane + 1, :]
-        tsend[way, 38:39, :] = fl
+        pack(way, 0, v_ref, plane, 18)
+        pack(way, 18, p_ref, plane, 9)
+        pack(way, 39, v_ref, plane, 9, 18)
+        tsend[way, 27:28, :] = df[plane:plane + 1, :]
+        tsend[way, 28:29, :] = mv[plane:plane + 1, :]
+        tsend[way, 29:30, :] = fl
     for i, (dt, ds) in enumerate(DIAG):
         way = 0 if dt > 0 else 1
         c0 = cells - 128 if ds > 0 else 0
@@ -99,8 +101,10 @@
 
     pl.semaphore_wait(barrier, jnp.where((s > 0) & (s < n_span - 1), 8, 5))
 
-    m1 = [remote(tsend.at[w, 0:32], trecv.at[w, 0:32], w, 1 - 2 * w, 0) for w in range(2)]
-    m2 = [remote(tsend.at[w, 32:48], trecv.at[w, 32:48], 2 + w, 1 - 2 * w, 0) for w in range(2)]
+    m1 = [remote(tsend.at[w, 0:24], trecv.at[w, 0:24], w, 1 - 2 * w, 0) for w in range(2)]
+    m2 = [remote(tsend.at[w, 24:40], trecv.at[w, 24:40], 2 + w, 1 - 2 * w, 0) for w in range(2)]
+    last = 10 + len(DIRS)
+    m3 = [remote(tsend.at[w, 40:48], trecv.at[w, 40:48], last + w, 1 - 2 * w, 0) for w in range(2)]
     ms = [remote(ssend.at[w], srecv.at[w], 4 + w, 0, 1 - 2 * w) for w in range(2)]
     md = [remote(dsend.at[i], drecv.at[i], 6 + i, dt, ds) for i, (dt, ds) in enumerate(DIAG)]
     mb = [remote(bsend, brecv.at[i], 10 + i, dt, ds) if ds == 0 else
@@ -164,7 +168,7 @@
 
         if c == 0:
             for way, plane in ((0, 7), (1, 0)):
-                pack(way, 39, pred_ref, plane, 9)
+                pack(way, 30, pred_ref, plane, 9)
                 m2[way].start()
         if c == 1:
             def columns(n, _):
@@ -199,19 +203,21 @@
 
     for m in m1 + m2:
         m.wait_recv()
+    for m in m3:
+        m.start()
     for m, (dt, ds) in zip(md, DIAG):
         there(-ds, m.wait_recv)
     for m, ds in zip(ms, (1, -1)):
         there(-ds, m.wait_recv)
 
-    df_dn, fl_dn = trecv[0, 36:37, :], trecv[0, 38:39, :]
-    df_up, fl_up = trecv[1, 36:37, :], trecv[1, 38:39, :]
+    df_dn, fl_dn = trecv[0, 27:28, :], trecv[0, 29:30, :]
+    df_up, fl_up = trecv[1, 27:28, :], trecv[1, 29:30, :]
     lo, hi = lane == 0, lane == cells - 1
-    edge0[0] = (trecv[0, 39:48, :] + df_dn * tsend[1, 0:9, :] - 0.1 * fl_dn * tsend[1, 27:36, :]
+    edge0[0] = (trecv[0, 30:39, :] + df_dn * tsend[1, 0:9, :] - 0.1 * fl_dn * tsend[1, 18:27, :]
                 + jnp.where(lo, df_dn * drecv[0, 0:9, 0:1], 0.0)
                 + jnp.where(hi, df_dn * drecv[1, 0:9, 0:1], 0.0))
-    edge0[1] = (trecv[1, 39:48, :] + (df_up + 0.1 * fl_up) * tsend[0, 0:9, :]
-                + 0.1 * fl_up * tsend[0, 27:36, :]
+    edge0[1] = (trecv[1, 30:39, :] + (df_up + 0.1 * fl_up) * tsend[0, 0:9, :]
+                + 0.1 * fl_up * tsend[0, 18:27, :]
                 + jnp.where(lo, df_up * drecv[2, 0:9, 0:1], 0.0)
                 + jnp.where(hi, df_up * drecv[3, 0:9, 0:1], 0.0))
     w_dn = jnp.where(row8 == 0, df + 0.1 * fl, 0.0)
@@ -221,11 +227,11 @@
 
     def completed(n, c, left, right):
         i = c * NT + n
-        out = (pred_ref[tile(i), :] + w_dn * trecv[0, pl.ds(i, 1), :]
-               + w_up * trecv[1, pl.ds(i, 1), :])
+        halo = pl.ds(i if c < 2 else 39 + n, 1)
+        out = pred_ref[tile(i), :] + w_dn * trecv[0, halo, :] + w_up * trecv[1, halo, :]
         if c == 0:
-            out = (out + q_dn * trecv[0, pl.ds(27 + n, 1), :]
-                   - q_up * trecv[1, pl.ds(27 + n, 1), :])
+            out = (out + q_dn * trecv[0, pl.ds(18 + n, 1), :]
+                   - q_up * trecv[1, pl.ds(18 + n, 1), :])
         ends = []
         for c0, col, side, sign in ((0, 0, left, 0.1), (cells - 128, 127, right, -0.1)):
             at = slice(c0, c0 + 128)
@@ -286,8 +292,8 @@
     kept, gone = [], []
     for w, plane in ((0, 0), (1, 7)):
         x = jnp.concatenate([sm_ref[8 * i + plane:8 * i + plane + 1, :] for i in range(NT)], 0)
-        x = x * trecv[w, 38:39, :]
-        g = x * trecv[w, 37:38, :]
+        x = x * trecv[w, 29:30, :]
+        g = x * trecv[w, 28:29, :]
         for rows, y in ((kept, x - g), (gone, g)):
             for z in pieces(y):
                 rows += [z, zero7]
@@ -329,7 +335,9 @@
         completed(n, 2, srecv[0, tile(n), :], srecv[1, tile(n), :])
         return 0
 
-    lax.fori_loop(0, NT, third_component, 0)
+    for m in m3:
+        m.wait_recv()
+    lax.fori_loop(0, NT, third_component, 0, unroll=3)
     for m, (dt, ds) in zip(mb, DIRS):
         there(-ds, m.wait_recv)
 
@@ -380,7 +388,7 @@
         top = mine.astype(BF16).astype(F32)
         lhs[n * 8:n * 8 + 8, :] = jnp.concatenate([top, mine - top], 1)
 
-    for m in m1 + m2:
+    for m in m1 + m2 + m3:
         m.wait_send()
     for m, ds in list(zip(ms, (1, -1))) + [(m, d[1]) for m, d in zip(md, DIAG)] + [
             (m, d[1]) for m, d in zip(mb, DIRS)]:
@@ -463,8 +471,8 @@
             pltpu.VMEM((128, cells), BF16),
             pltpu.VMEM((128, cells), BF16),
             pltpu.VMEM((2, 9, cells), F32),
-            pltpu.SemaphoreType.DMA((10 + n,)),
-            pltpu.SemaphoreType.DMA((10 + n,)),
+            pltpu.SemaphoreType.DMA((12 + n,)),
+            pltpu.SemaphoreType.DMA((12 + n,)),
             pltpu.SemaphoreType.DMA((7,)),
         ],
         compiler_params=pltpu.CompilerParams(

time: 26.8 us -> 25.4 us (0.948)
  Pallas kernels: 25.3 us -> 23.9 us
    pallas_call x1, Pallas kernels: 23.2 us -> 21.8 us  [shards(): pl.pallas_call(functools.partial(kernel, n_theta, n_span), out_shape=(jax...]
where the time goes in v4:
time: 25.4 us; the launch traced here: 25.2 us
  Pallas kernels  23.9 us (94%)
  between operations  1.29 us (5%)
    pallas_call x1, Pallas kernels, shards(): pl.pallas_call(functools.partial(kernel, n_theta, n_span), out_shape=(jax...  21.8 us
    pallas_call x1, Pallas kernels, shards(): pl.pallas_call(lift_kernel, out_shape=(jax.ShapeDtypeStruct((ncomp * rows...  2.12 us

profile of v4, /device:TPU:0, one launch (start us, length us, event | category | flops | bytes accessed | tf_op | source)
XLA Modules:
  0.0 25.2 jit_solution(15000268470837725222)
XLA Ops:
  1.3 21.8 %shard_map.77 = (f32[216,2048]{1,0:T(8,128)S(1)}, f32[72,2048]{1,0:T(8,128)S(1)}, f32[72,256]{1,0:T(8,128)S(1)}) custom-call(s32[1,1]{1,0:T(1,128)S(6)} %copy.8.live_ref, f32[216,2048]{1,0:T(8,128)} %bitcast.4, f32[72,2048]{1,0:T(8,128)} %bitcast.5, f32[8,2048]{1,0:T(8,128)} %d_hbm.1, s32[8,2048]{1,0:T(8,128)} %own_hbm.3, f32[2,128]{1,0:T(2,128)} %cd_hbm.1), custom_call_target="tpu_custom_call" | custom-call | tf_op jit(solution)/shard_map/pallas_call | solution.py:443
  23.1 2.1 %shard_map.78 = (f32[216,2048]{1,0:T(8,128)}, f32[72,2048]{1,0:T(8,128)}) custom-call(s32[1,1]{1,0:T(1,128)S(6)} %copy.8.live_ref, f32[216,2048]{1,0:T(8,128)S(1)} %get-tuple-element.7.raw_ref, f32[72,2048]{1,0:T(8,128)S(1)} %get-tuple-element.8.sm_ref, f32[72,256]{1,0:T(8,128)S(1)} %get-tuple-element.9.lhs, s32[8,2048]{1,0:T(8,128)} %own_hbm.3), custom_call_target="tpu_custom_call" | custom-call | tf_op jit(solution)/shard_map/pallas_call | solution.py:486

commit v5 on v4

--- a/solution.py
+++ b/solution.py
@@ -201,25 +201,12 @@
 
     lax.fori_loop(0, cells // width, members, 0)
 
-    for m in m1 + m2:
+    for m in m1:
         m.wait_recv()
-    for m in m3:
-        m.start()
     for m, (dt, ds) in zip(md, DIAG):
         there(-ds, m.wait_recv)
     for m, ds in zip(ms, (1, -1)):
         there(-ds, m.wait_recv)
-
-    df_dn, fl_dn = trecv[0, 27:28, :], trecv[0, 29:30, :]
-    df_up, fl_up = trecv[1, 27:28, :], trecv[1, 29:30, :]
-    lo, hi = lane == 0, lane == cells - 1
-    edge0[0] = (trecv[0, 30:39, :] + df_dn * tsend[1, 0:9, :] - 0.1 * fl_dn * tsend[1, 18:27, :]
-                + jnp.where(lo, df_dn * drecv[0, 0:9, 0:1], 0.0)
-                + jnp.where(hi, df_dn * drecv[1, 0:9, 0:1], 0.0))
-    edge0[1] = (trecv[1, 30:39, :] + (df_up + 0.1 * fl_up) * tsend[0, 0:9, :]
-                + 0.1 * fl_up * tsend[0, 18:27, :]
-                + jnp.where(lo, df_up * drecv[2, 0:9, 0:1], 0.0)
-                + jnp.where(hi, df_up * drecv[3, 0:9, 0:1], 0.0))
     w_dn = jnp.where(row8 == 0, df + 0.1 * fl, 0.0)
     w_up = jnp.where(row8 == 7, df, 0.0)
     q_dn = jnp.where(row8 == 0, 0.1 * fl, 0.0)
@@ -243,10 +230,31 @@
         pred_ref[tile(i), :] = out
         return out
 
+    def second_component(n, _):
+        completed(n, 1, srecv[0, tile(n), :], srecv[1, tile(n), :])
+        return 0
+
+    lax.fori_loop(0, NT, second_component, 0, unroll=3)
+    for m in m2:
+        m.wait_recv()
+    for m in m3:
+        m.start()
+
+    df_dn, fl_dn = trecv[0, 27:28, :], trecv[0, 29:30, :]
+    df_up, fl_up = trecv[1, 27:28, :], trecv[1, 29:30, :]
+    lo, hi = lane == 0, lane == cells - 1
+    edge0[0] = (trecv[0, 30:39, :] + df_dn * tsend[1, 0:9, :] - 0.1 * fl_dn * tsend[1, 18:27, :]
+                + jnp.where(lo, df_dn * drecv[0, 0:9, 0:1], 0.0)
+                + jnp.where(hi, df_dn * drecv[1, 0:9, 0:1], 0.0))
+    edge0[1] = (trecv[1, 30:39, :] + (df_up + 0.1 * fl_up) * tsend[0, 0:9, :]
+                + 0.1 * fl_up * tsend[0, 18:27, :]
+                + jnp.where(lo, df_up * drecv[2, 0:9, 0:1], 0.0)
+                + jnp.where(hi, df_up * drecv[3, 0:9, 0:1], 0.0))
+
     def complete(n, _):
         left, right = srecv[0, tile(n), :], srecv[1, tile(n), :]
         first = completed(n, 0, left, right)
-        second = completed(n, 1, left, right)
+        second = pred_ref[tile(NT + n), :]
         fp = jnp.where(row8 == 7, edge0[1, pl.ds(n, 1), :], pltpu.roll(first, 7, 0))
         fm = jnp.where(row8 == 0, edge0[0, pl.ds(n, 1), :], pltpu.roll(first, 1, 0))
         x = [v_ref[tile(NT + n), 0:128][:, 0:1],
@@ -399,8 +407,11 @@
     cells = own_ref.shape[1]
     width = 256
     count = cells // width
-    pred_out = pltpu.make_async_copy(raw_ref, pred_hbm, sems.at[0])
-    pred_out.start()
+    piece = raw_ref.shape[0] // 3
+    pred_out = [pltpu.make_async_copy(raw_ref.at[piece * c:piece * c + piece], pred_hbm.at[piece * c:piece * c + piece],
+                                      sems.at[6 + c]) for c in range(3)]
+    for m in pred_out:
+        m.start()
     own_in = pltpu.make_async_copy(own_hbm, own_ref, sems.at[1])
     own_in.start()
     first = lax.axis_index("span") * (cells // FAN)
@@ -427,7 +438,7 @@
             at = slice(j * width - width, j * width + width)
             outs.append(pltpu.make_async_copy(corr.at[:, at], corr_hbm.at[:, at], sems.at[2 + j // 2]))
             outs[-1].start()
-    for m in outs + [pred_out]:
+    for m in outs + pred_out:
         m.wait()
 
 
@@ -494,7 +505,7 @@
         scratch_shapes=[
             pltpu.VMEM((planes, cells), jnp.int32),
             pltpu.VMEM((rows, cells), F32),
-            pltpu.SemaphoreType.DMA((8,)),
+            pltpu.SemaphoreType.DMA((9,)),
         ],
         compiler_params=pltpu.CompilerParams(vmem_limit_bytes=24 * 2**20),
     )(live, raw, sm, lhs, own)

time: 25.4 us -> 25 us (0.984)
  Pallas kernels: 23.9 us -> 23.5 us
    pallas_call x1, Pallas kernels: 21.8 us -> 21.4 us  [shards(): pl.pallas_call(functools.partial(kernel, n_theta, n_span), out_shape=(jax...]
where the time goes in v5:
time: 25 us; the launch traced here: 24.8 us
  Pallas kernels  23.5 us (94%)
  between operations  1.29 us (5%)
    pallas_call x1, Pallas kernels, shards(): pl.pallas_call(functools.partial(kernel, n_theta, n_span), out_shape=(jax...  21.4 us
    pallas_call x1, Pallas kernels, shards(): pl.pallas_call(lift_kernel, out_shape=(jax.ShapeDtypeStruct((ncomp * rows...  2.14 us

profile of v5, /device:TPU:0, one launch (start us, length us, event | category | flops | bytes accessed | tf_op | source)
XLA Modules:
  0.0 24.8 jit_solution(12992952911426078664)
XLA Ops:
  1.3 21.4 %shard_map.77 = (f32[216,2048]{1,0:T(8,128)S(1)}, f32[72,2048]{1,0:T(8,128)S(1)}, f32[72,256]{1,0:T(8,128)S(1)}) custom-call(s32[1,1]{1,0:T(1,128)S(6)} %copy.8.live_ref, f32[216,2048]{1,0:T(8,128)} %bitcast.4, f32[72,2048]{1,0:T(8,128)} %bitcast.5, f32[8,2048]{1,0:T(8,128)} %d_hbm.1, s32[8,2048]{1,0:T(8,128)} %own_hbm.3, f32[2,128]{1,0:T(2,128)} %cd_hbm.1), custom_call_target="tpu_custom_call" | custom-call | tf_op jit(solution)/shard_map/pallas_call | solution.py:454
  22.7 2.1 %shard_map.78 = (f32[216,2048]{1,0:T(8,128)}, f32[72,2048]{1,0:T(8,128)}) custom-call(s32[1,1]{1,0:T(1,128)S(6)} %copy.8.live_ref, f32[216,2048]{1,0:T(8,128)S(1)} %get-tuple-element.7.raw_ref, f32[72,2048]{1,0:T(8,128)S(1)} %get-tuple-element.8.sm_ref, f32[72,256]{1,0:T(8,128)S(1)} %get-tuple-element.9.lhs, s32[8,2048]{1,0:T(8,128)} %own_hbm.3), custom_call_target="tpu_custom_call" | custom-call | tf_op jit(solution)/shard_map/pallas_call | solution.py:497
